TPU v7x, 128 devices: a whole 4x4x4 slice. The times are simulated.
128 devices in a mesh: lon: 32 (over z, y, core), lat: 4 (over x).
Axes of the slice: x: 4, y: 4, z: 4, core: 2. Of those that a mesh axis runs over, the one named last changes fastest.
Arguments:
- node_latent: bfloat16 [32768, 512], P(('lon', 'lat')), may hold values from -6 to 6
- edge_latent: bfloat16 [262144, 512], P(('lon', 'lat')), may hold values from -6 to 6
- edge_sender: int32 [262144], P(('lon', 'lat')), may hold values from 0 to 511
- edge_receiver: int32 [262144], P(('lon', 'lat')), may hold values from 0 to 255, as said below
- edge_count: int32 [128], P(('lon', 'lat')), may hold values from 256 to 2048, as said below
- halo_send: int32 [128, 4, 64], P(('lon', 'lat')), may hold values from 0 to 255
- weight_in: bfloat16 [1536, 512], replicated, may hold values from -0.15625 to 0.15625
- bias_in: float32 [512], replicated, may hold values from -3 to 3
- weight_out: bfloat16 [512, 512], replicated, may hold values from -0.25 to 0.25
- bias_out: float32 [512], replicated, may hold values from -3 to 3
- norm_gain: float32 [512], replicated, may hold values from 0.5 to 1.5
- edge_cotangent: bfloat16 [262144, 512], P(('lon', 'lat')), may hold values from -6 to 6
- node_cotangent: bfloat16 [32768, 512], P(('lon', 'lat')), may hold values from -6 to 6
Outputs:
- edge_grad: bfloat16 [262144, 512], P(('lon', 'lat'))
- node_grad: bfloat16 [32768, 512], P(('lon', 'lat'))
- grad_w_in: float32 [1536, 512], replicated
- grad_b_in: float32 [512], replicated
- grad_w_out: float32 [512, 512], replicated
- grad_b_out: float32 [512], replicated
- grad_gain: float32 [512], replicated
Inputs may be any that keep to these rules, and one draw needn't show every extreme that they name: `edge_receiver`: within each partition's block of 2048 entries the values never fall. `edge_count`: some partition is full in every draw.
All inputs are finite; a program needn't handle non-finite values.
Results may differ from a plain program's by a relative error of at most 0.0047.
Values may be sent and summed in bfloat16 or wider, within the bound.
A program may use at most 128 MiB of HBM per device.

v0:
```python
import jax
import jax.numpy as jnp
from jax import lax
from jax.sharding import PartitionSpec as P


def passed_along(value, axis, by):
    size = lax.axis_size(axis)
    return lax.ppermute(value, axis, [(i, (i + by) % size) for i in range(size)])


def passed_along_2(value, axis, steps):
    count = lax.axis_size(axis)
    leading, last = (max(0, -steps), min(count, count - steps))
    return lax.ppermute(value, axis, [(source, source + steps) for source in range(leading, last)])


def one_hot_rows(index, count):
    return (index[:, None] == jnp.arange(count, dtype=jnp.int32)[None, :]).astype(jnp.bfloat16)


def pick_by_table(onehot, values):
    return jnp.dot(onehot, values, preferred_element_type=jnp.float32).astype(jnp.bfloat16)


def add_by_table(onehot, values):
    return lax.dot_general(
        onehot.astype(jnp.float32),
        values,
        (((0,), (0,)), ((), ())),
        precision=lax.Precision.HIGHEST,
        preferred_element_type=jnp.float32,
    )


def edge_backward(
    ext,
    edge_lat,
    sender,
    receiver,
    count,
    edge_cot,
    node_cot,
    weight_in,
    bias_in,
    weight_out,
    bias_out,
    norm_gain,
):
    n_edges = edge_lat.shape[0]
    width = edge_lat.shape[1]
    node_rows = node_cot.shape[0]
    ext_rows = ext.shape[0]
    live = (jnp.arange(n_edges, dtype=jnp.int32) < count).astype(jnp.float32)[:, None]
    sender_table = one_hot_rows(sender, ext_rows)
    receiver_table = one_hot_rows(receiver, node_rows)
    joined = jnp.concatenate(
        [
            edge_lat,
            pick_by_table(sender_table, ext),
            pick_by_table(receiver_table, ext[:node_rows]),
        ],
        axis=1,
    )
    pre = jnp.dot(joined, weight_in, preferred_element_type=jnp.float32) + bias_in
    sig = jax.nn.sigmoid(pre)
    act = (pre * sig).astype(jnp.bfloat16)
    mixed = jnp.dot(act, weight_out, preferred_element_type=jnp.float32) + bias_out
    centred = mixed - jnp.mean(mixed, axis=1, keepdims=True)
    scale = lax.rsqrt(jnp.mean(centred * centred, axis=1, keepdims=True) + 1e-05)
    normed = centred * scale
    node_part = jnp.dot(receiver_table, node_cot, preferred_element_type=jnp.float32)
    upstream = live * (edge_cot.astype(jnp.float32) + node_part)
    grad_gain = jnp.sum(upstream * normed, axis=0)
    scaled = upstream * norm_gain
    d_mixed = scale * (
        scaled
        - jnp.mean(scaled, axis=1, keepdims=True)
        - normed * jnp.mean(scaled * normed, axis=1, keepdims=True)
    )
    d_mixed_b = d_mixed.astype(jnp.bfloat16)
    grad_b_out = jnp.sum(d_mixed, axis=0)
    grad_w_out = lax.dot_general(
        act, d_mixed_b, (((0,), (0,)), ((), ())), preferred_element_type=jnp.float32
    )
    d_act = lax.dot_general(
        d_mixed_b, weight_out, (((1,), (1,)), ((), ())), preferred_element_type=jnp.float32
    )
    d_pre = d_act * sig * (1.0 + pre * (1.0 - sig))
    d_pre_b = d_pre.astype(jnp.bfloat16)
    grad_b_in = jnp.sum(d_pre, axis=0)
    grad_w_in = lax.dot_general(
        joined, d_pre_b, (((0,), (0,)), ((), ())), preferred_element_type=jnp.float32
    )
    d_joined = lax.dot_general(
        d_pre_b, weight_in, (((1,), (1,)), ((), ())), preferred_element_type=jnp.float32
    )
    edge_grad = (live * (edge_cot.astype(jnp.float32) + d_joined[:, :width])).astype(jnp.bfloat16)
    table = add_by_table(sender_table, d_joined[:, width : 2 * width])
    at_receivers = add_by_table(receiver_table, d_joined[:, 2 * width :])
    table = table.at[:node_rows].add(at_receivers)
    return (edge_grad, table, (grad_w_in, grad_b_in, grad_w_out, grad_b_out, grad_gain))


def body(
    node_latent,
    edge_latent,
    edge_sender,
    edge_receiver,
    edge_count,
    halo_send,
    weight_in,
    bias_in,
    weight_out,
    bias_out,
    norm_gain,
    edge_cotangent,
    node_cotangent,
):
    node_rows = node_latent.shape[0]
    width = node_latent.shape[1]
    lists = halo_send[0]
    halo_rows = lists.shape[1]
    flat_lists = lists.reshape(-1)
    list_table = one_hot_rows(flat_lists, node_rows)
    rows = pick_by_table(list_table, node_latent).reshape(4, halo_rows, width)
    moved = []
    for position, by in ((0, 1), (1, -1)):
        moved.append(passed_along(rows[position], "lon", by))
    for position, by in ((2, 1), (3, -1)):
        moved.append(passed_along_2(rows[position], "lat", by))
    slots = jnp.stack(moved)
    ext = jnp.concatenate([node_latent, slots.reshape(4 * halo_rows, width)], axis=0)
    edge_grad, table, sums = edge_backward(
        ext,
        edge_latent,
        edge_sender,
        edge_receiver,
        edge_count[0],
        edge_cotangent,
        node_cotangent,
        weight_in,
        bias_in,
        weight_out,
        bias_out,
        norm_gain,
    )
    halo_grads = table[node_rows:].reshape(4, halo_rows, width).astype(jnp.bfloat16)
    returns = []
    for position, by in ((0, -1), (1, 1)):
        returns.append(passed_along(halo_grads[position], "lon", by))
    for position, by in ((2, -1), (3, 1)):
        returns.append(passed_along_2(halo_grads[position], "lat", by))
    back = jnp.stack(returns)
    added = lax.dot_general(
        list_table,
        back.reshape(4 * halo_rows, width),
        (((0,), (0,)), ((), ())),
        preferred_element_type=jnp.float32,
    )
    node_grad = table[:node_rows] + added
    grad_w_in, grad_b_in, grad_w_out, grad_b_out, grad_gain = lax.psum(
        (sums[0], sums[1], sums[2], sums[3], sums[4]), ("lon", "lat")
    )
    return (
        edge_grad,
        node_grad.astype(jnp.bfloat16),
        grad_w_in,
        grad_b_in,
        grad_w_out,
        grad_b_out,
        grad_gain,
    )


def solution(mesh):
    return jax.shard_map(
        body,
        mesh=mesh,
        in_specs=(
            P(("lon", "lat"), None),
            P(("lon", "lat"), None),
            P(("lon", "lat")),
            P(("lon", "lat")),
            P(("lon", "lat")),
            P(("lon", "lat"), None, None),
            P(),
            P(),
            P(),
            P(),
            P(),
            P(("lon", "lat"), None),
            P(("lon", "lat"), None),
        ),
        out_specs=(P(("lon", "lat"), None), P(("lon", "lat"), None), P(), P(), P(), P(), P()),
        check_vma=False,
    )
```

profile of v0, /device:TPU:1, one launch (start us, length us, event | category | flops | bytes accessed | tf_op | source)
XLA Modules:
  0.0 227.7 jit_solution(17922922557432205687)
XLA Ops:
  9.4 2.8 %collective-permute-start = (bf16[64,512]{1,0:T(8,128)(2,1)S(1)}, bf16[64,512]{1,0:T(8,128)(2,1)S(1)}, u32[]{:S(2)}, u32[]{:S(2)}) collective-permute-start(bf16[64,512]{1,0:T(8,128)(2,1)S(1)} %get-tuple-element.40), channel_id=1, source_target_pairs={{0,4},{4,8},{8,12},{12,16},{16,20},{20,24},{24,28},{28,32},{32,36}... | collective-permute-start | bytes 196616 | tf_op jit(solution)/shard_map/ppermute | solution.py:9
  12.1 3.1 %collective-permute-start.2 = (bf16[64,512]{1,0:T(8,128)(2,1)S(1)}, bf16[64,512]{1,0:T(8,128)(2,1)S(1)}, u32[]{:S(2)}, u32[]{:S(2)}) collective-permute-start(bf16[64,512]{1,0:T(8,128)(2,1)S(1)} %get-tuple-element.42), channel_id=1, source_target_pairs={{0,1},{1,2},{2,3},{4,5},{5,6},{6,7},{8,9},{9,10},{10,11},{12,13},{... | collective-permute-start | bytes 196616 | tf_op jit(solution)/shard_map/ppermute | solution.py:15
  16.5 3.2 %convolution_convert_fusion = bf16[2048,512]{0,1:T(8,128)(2,1)} fusion(bf16[256,512]{1,0:T(8,128)(2,1)} %param.15, s32[2048]{0:T(1024)} %param.18), kind=kOutput, calls=%fused_computation.23 | convolution fusion | flops 538443776 | bytes 2367488 | tf_op jit(solution)/shard_map/dot_general | solution.py:23
  19.7 4.0 %copy.21 = bf16[2048,512]{0,1:T(8,128)(2,1)} copy(bf16[2048,512]{1,0:T(8,128)(2,1)} %param.16) | data formatting | bytes 4194304 | tf_op args[1]
  23.7 4.0 %copy.20 = bf16[2048,512]{0,1:T(8,128)(2,1)} copy(bf16[2048,512]{1,0:T(8,128)(2,1)} %param.26) | data formatting | bytes 4194304 | tf_op args[11]
  30.5 3.5 %fusion.10 = f32[2048,512]{1,0:T(8,128)S(1)} fusion(bf16[1536,512]{1,0:T(8,128)(2,1)S(1)} %copy-done, bf16[2048,512]{0,1:T(8,128)(2,1)S(1)} %copy-done.2, bf16[2048,512]{0,1:T(8,128)(2,1)S(1)} %fusion.8, bf16[2048,512]{0,1:T(8,128)(2,1)S(1)} %copy-done.4), kind=kOutput, calls=%fused_computation.25 | convolution fusion | flops 3240099840 | bytes 12058624 | tf_op jit(solution)/shard_map/dot_general | solution.py:65
  37.4 3.1 %multiply_reduce_fusion = (f32[512]{0:T(512)}, f32[2048]{0:T(1024)S(1)}, f32[2048]{0:T(1024)S(1)}, f32[2048,512]{0,1:T(8,128)S(1)}) fusion(f32[2048,512]{0,1:T(8,128)S(1)} %get-tuple-element.45, f32[2048]{0:T(1024)S(1)} %add_rsqrt_fusion, f32[2048]{0:T(1024)S(1)} %broadcast_multiply_fusion.2, f32[512]{0:T(512)S(1)} %copy-done.10, f32[512]{0:T(512)S(1)} %copy-done.14, ...), kind=kOutput, calls=%fused_computation.10 | convolution fusion | flops 549973504 | bytes 10803200 | tf_op jit(solution)/shard_map/dot_general | solution.py:72
  40.5 2.6 %fusion.36 = (f32[512]{0:T(512)}, bf16[2048,512]{0,1:T(8,128)(2,1)S(1)}) fusion(f32[2048]{0:T(1024)S(1)} %get-tuple-element.51, f32[2048]{0:T(1024)S(1)} %broadcast_multiply_fusion.2, f32[2048,512]{0,1:T(8,128)S(1)} %get-tuple-element.45, f32[512]{0:T(512)S(1)} %copy-done.10, f32[2048]{0:T(1024)S(1)} %get-tuple-element.52, ...), kind=kLoop, calls=%fused_computation.60 | loop fusion | flops 10485248 | bytes 10524672 | tf_op jit(solution)/shard_map/reduce_sum | solution.py:82
  43.0 3.4 %fusion.40 = (f32[512]{0:T(512)}, bf16[2048,512]{1,0:T(8,128)(2,1)S(1)}) fusion(f32[2048,512]{1,0:T(8,128)S(1)} %fusion.10, f32[512]{0:T(512)S(1)} %copy-done.18, bf16[512,512]{1,0:T(8,128)(2,1)S(1)} %copy-done.15, bf16[2048,512]{0,1:T(8,128)(2,1)S(1)} %get-tuple-element.35), kind=kOutput, calls=%fused_computation.64 | convolution fusion | flops 1085275648 | bytes 8916992 | tf_op jit(solution)/shard_map/dot_general | solution.py:86
  46.4 2.3 %fusion.20 = f32[512,512]{1,0:T(8,128)} fusion(bf16[2048,512]{0,1:T(8,128)(2,1)S(1)} %get-tuple-element.35, f32[2048,512]{1,0:T(8,128)S(1)} %fusion.10, f32[512]{0:T(512)S(1)} %copy-done.18), kind=kOutput, calls=%fused_computation.36 | convolution fusion | flops 1080033280 | bytes 7342080 | tf_op jit(solution)/shard_map/dot_general | solution.py:83
  48.8 8.8 %fusion.9 = f32[1536,512]{1,0:T(8,128)} fusion(bf16[2048,512]{0,1:T(8,128)(2,1)S(1)} %copy-done.2, bf16[2048,512]{0,1:T(8,128)(2,1)S(1)} %fusion.8, bf16[2048,512]{0,1:T(8,128)(2,1)S(1)} %copy-done.4, bf16[2048,512]{1,0:T(8,128)(2,1)S(1)} %get-tuple-element.50), kind=kOutput, calls=%fused_computation.24 | convolution fusion | flops 3240099840 | bytes 11534336 | tf_op jit(solution)/shard_map/dot_general | solution.py:92
  57.6 5.2 %fusion.18 = f32[2048,1536]{1,0:T(8,128)S(1)} fusion(bf16[1536,512]{1,0:T(8,128)(2,1)S(1)} %copy-done, bf16[2048,512]{1,0:T(8,128)(2,1)} %copy-done.19), kind=kOutput, calls=%fused_computation.34 | convolution fusion | flops 3221225472 | bytes 16252928 | tf_op jit(solution)/shard_map/dot_general | solution.py:95
  62.8 2.7 %slice.83 = f32[2048,512]{1,0:T(8,128)} slice(f32[2048,1536]{1,0:T(8,128)S(1)} %fusion.18), slice={[0:2048], [0:512]} | slice | bytes 8388608 | tf_op jit(solution)/shard_map/slice | solution.py:98
  65.5 3.1 %copy-done.3 = f32[2048,1536]{1,0:T(8,128)} copy-done((f32[2048,1536]{1,0:T(8,128)}, f32[2048,1536]{1,0:T(8,128)S(1)}, u32[]{:S(2)}) %copy-start.3) | copy-done | bytes 12582936
  68.6 4.0 %fusion.39 = (bf16[512,512]{1,0:T(8,128)(2,1)S(1)}, f32[512,512]{1,0:T(8,128)S(1)}) fusion(f32[2048,1536]{1,0:T(8,128)S(1)} %fusion.18, s32[2048]{0:T(1024)S(1)} %copy-done.17), kind=kOutput, calls=%fused_computation.63 | convolution fusion | flops 6443761664 | bytes 5775360 | tf_op jit(solution)/shard_map/dot_general | solution.py:27
  73.3 5.1 %collective-permute-start.4 = (bf16[64,512]{1,0:T(8,128)(2,1)}, bf16[64,512]{1,0:T(8,128)(2,1)S(1)}, u32[]{:S(2)}, u32[]{:S(2)}) collective-permute-start(bf16[64,512]{1,0:T(8,128)(2,1)} %get-tuple-element.36), channel_id=1, source_target_pairs={{0,124},{4,0},{8,4},{12,8},{16,12},{20,16},{24,20},{28,24},{32,28}... | collective-permute-start | bytes 196616 | tf_op jit(solution)/shard_map/ppermute | solution.py:9
  79.7 5.6 %collective-permute-start.7 = (bf16[64,512]{1,0:T(8,128)(2,1)S(1)}, bf16[64,512]{1,0:T(8,128)(2,1)}, u32[]{:S(2)}, u32[]{:S(2)}) collective-permute-start(bf16[64,512]{1,0:T(8,128)(2,1)S(1)} %get-tuple-element.37), channel_id=1, source_target_pairs={{0,1},{1,2},{2,3},{4,5},{5,6},{6,7},{8,9},{9,10},{10,11},{12,13},{... | collective-permute-start | bytes 196616 | tf_op jit(solution)/shard_map/ppermute | solution.py:15
  85.3 5.4 %copy.26 = f32[2048,512]{0,1:T(8,128)} copy(f32[2048,512]{1,0:T(8,128)} %slice.83) | data formatting | bytes 8388608
  90.7 5.1 %fusion.2 = bf16[2048,512]{0,1:T(8,128)(2,1)} fusion(f32[2048,512]{0,1:T(8,128)} %copy.26, bf16[2048,512]{0,1:T(8,128)(2,1)} %copy.20, f32[2048]{0:T(1024)S(1)} %fusion.31), kind=kLoop, calls=%fused_computation.5 | loop fusion | flops 4194304 | bytes 8396800 | tf_op jit(solution)/shard_map/convert_element_type | solution.py:98
  95.8 5.0 %fusion.13 = f32[256,512]{1,0:T(8,128)S(1)} fusion(f32[2048,1536]{1,0:T(8,128)} %copy-done.3, s32[2048]{0:T(1024)S(1)} %copy-done.7, f32[512,512]{1,0:T(8,128)S(1)} %get-tuple-element.48), kind=kOutput, calls=%fused_computation.30 | convolution fusion | flops 3221880832 | bytes 5251072 | tf_op jit(solution)/shard_map/dot_general | solution.py:27
  100.8 3.9 %copy.24 = bf16[2048,512]{1,0:T(8,128)(2,1)} copy(bf16[2048,512]{0,1:T(8,128)(2,1)} %fusion.2) | data formatting | bytes 4194304
  104.8 65.4 %all-reduce = (f32[512]{0:T(512)}, f32[512]{0:T(512)}, f32[512]{0:T(512)}) all-reduce(f32[512]{0:T(512)S(1)} %copy-done.13, f32[512]{0:T(512)S(1)} %copy-done.11, f32[512]{0:T(512)S(1)} %copy-done.12), channel_id=1, replica_groups=mesh['lon'=32,'lat'=4] {'lon','lat'}, use_global_device_ids=true, to_apply=%region_6.0 | all-reduce | flops 1536 | bytes 12288 | tf_op jit(solution)/shard_map/psum | solution.py:162
  172.2 43.7 %all-reduce.4.cloned.1.call-done = (f32[1536,512]{1,0:T(8,128)}, f32[512,512]{1,0:T(8,128)}) async-done(((f32[1536,512]{1,0:T(8,128)}, f32[512,512]{1,0:T(8,128)}), (f32[1536,512]{1,0:T(8,128)}, f32[512,512]{1,0:T(8,128)})) %all-reduce.4.cloned.1.call-update) | async-done | bytes 4194320 | tf_op jit(solution)/shard_map/psum | solution.py:162
  215.9 3.9 %copy.30 = f32[1536,512]{1,0:T(8,128)} copy(f32[1536,512]{1,0:T(8,128)} %get-tuple-element.59) | data formatting | bytes 6291456
  (68 shorter events, 13.6 us)
Async XLA Ops:
  7.2 23.3 %copy-start = (bf16[1536,512]{1,0:T(8,128)(2,1)S(1)}, bf16[1536,512]{1,0:T(8,128)(2,1)}, u32[]{:S(2)}) copy-start(bf16[1536,512]{1,0:T(8,128)(2,1)} %param.21) | copy-start | bytes 4718596
  7.2 208.7 %all-reduce.4.cloned.1.call-start = ((), (), s32[]{:S(2)}) async-start(), calls=%async_computation | async-start | bytes 8388608 | tf_op jit(solution)/shard_map/psum | solution.py:162
  8.1 8.4 %copy-start.8 = (s32[256]{0:T(256)}, s32[256]{0:T(256)S(1)}, u32[]{:S(2)}) copy-start(s32[256]{0:T(256)S(1)} %eq.44) | copy-start | bytes 3076
  9.4 19.1 %collective-permute-start = (bf16[64,512]{1,0:T(8,128)(2,1)S(1)}, bf16[64,512]{1,0:T(8,128)(2,1)S(1)}, u32[]{:S(2)}, u32[]{:S(2)}) collective-permute-start(bf16[64,512]{1,0:T(8,128)(2,1)S(1)} %get-tuple-element.40), channel_id=1, source_target_pairs={{0,4},{4,8},{8,12},{12,16},{16,20},{20,24},{24,28},{28,32},{32,36}... | collective-permute-start | bytes 196616 | tf_op jit(solution)/shard_map/ppermute | solution.py:9
  12.1 16.4 %collective-permute-start.1 = (bf16[64,512]{1,0:T(8,128)(2,1)S(1)}, bf16[64,512]{1,0:T(8,128)(2,1)S(1)}, u32[]{:S(2)}, u32[]{:S(2)}) collective-permute-start(bf16[64,512]{1,0:T(8,128)(2,1)S(1)} %get-tuple-element.43), channel_id=1, source_target_pairs={{0,124},{4,0},{8,4},{12,8},{16,12},{20,16},{24,20},{28,24},{32,28}... | collective-permute-start | bytes 196616 | tf_op jit(solution)/shard_map/ppermute | solution.py:9
  12.1 16.4 %collective-permute-start.2 = (bf16[64,512]{1,0:T(8,128)(2,1)S(1)}, bf16[64,512]{1,0:T(8,128)(2,1)S(1)}, u32[]{:S(2)}, u32[]{:S(2)}) collective-permute-start(bf16[64,512]{1,0:T(8,128)(2,1)S(1)} %get-tuple-element.42), channel_id=1, source_target_pairs={{0,1},{1,2},{2,3},{4,5},{5,6},{6,7},{8,9},{9,10},{10,11},{12,13},{... | collective-permute-start | bytes 196616 | tf_op jit(solution)/shard_map/ppermute | solution.py:15
  15.2 13.3 %collective-permute-start.3 = (bf16[64,512]{1,0:T(8,128)(2,1)S(1)}, bf16[64,512]{1,0:T(8,128)(2,1)S(1)}, u32[]{:S(2)}, u32[]{:S(2)}) collective-permute-start(bf16[64,512]{1,0:T(8,128)(2,1)S(1)} %get-tuple-element.41), channel_id=1, source_target_pairs={{1,0},{2,1},{3,2},{5,4},{6,5},{7,6},{9,8},{10,9},{11,10},{13,12},{... | collective-permute-start | bytes 196616 | tf_op jit(solution)/shard_map/ppermute | solution.py:15
  19.7 8.8 %copy-start.5 = (bf16[256,512]{1,0:T(8,128)(2,1)S(1)}, bf16[256,512]{1,0:T(8,128)(2,1)}, u32[]{:S(2)}) copy-start(bf16[256,512]{1,0:T(8,128)(2,1)} %param.15) | copy-start | bytes 786436
  19.7 8.9 %copy-start.17 = (s32[2048]{0:T(1024)S(1)}, s32[2048]{0:T(1024)}, u32[]{:S(2)}) copy-start(s32[2048]{0:T(1024)} %param.17) | copy-start | bytes 24580
  27.6 2.8 %copy-start.2 = (bf16[2048,512]{0,1:T(8,128)(2,1)S(1)}, bf16[2048,512]{0,1:T(8,128)(2,1)}, u32[]{:S(2)}) copy-start(bf16[2048,512]{0,1:T(8,128)(2,1)} %convolution_convert_fusion) | copy-start | bytes 6291460
  27.7 2.8 %copy-start.4 = (bf16[2048,512]{0,1:T(8,128)(2,1)S(1)}, bf16[2048,512]{0,1:T(8,128)(2,1)}, u32[]{:S(2)}) copy-start(bf16[2048,512]{0,1:T(8,128)(2,1)} %copy.21) | copy-start | bytes 6291460
  30.5 3.5 %copy-start.10 = (f32[512]{0:T(512)S(1)}, f32[512]{0:T(512)}, u32[]{:S(2)}) copy-start(f32[512]{0:T(512)} %param.24) | copy-start | bytes 6148
  30.5 3.5 %copy-start.15 = (bf16[512,512]{1,0:T(8,128)(2,1)S(1)}, bf16[512,512]{1,0:T(8,128)(2,1)}, u32[]{:S(2)}) copy-start(bf16[512,512]{1,0:T(8,128)(2,1)} %param.23) | copy-start | bytes 1572868
  30.5 3.5 %copy-start.18 = (f32[512]{0:T(512)S(1)}, f32[512]{0:T(512)}, u32[]{:S(2)}) copy-start(f32[512]{0:T(512)} %param.22) | copy-start | bytes 6148
  62.8 5.8 %copy-start.3 = (f32[2048,1536]{1,0:T(8,128)}, f32[2048,1536]{1,0:T(8,128)S(1)}, u32[]{:S(2)}) copy-start(f32[2048,1536]{1,0:T(8,128)S(1)} %fusion.18) | copy-start | bytes 37748740
  73.3 96.9 %collective-permute-start.4 = (bf16[64,512]{1,0:T(8,128)(2,1)}, bf16[64,512]{1,0:T(8,128)(2,1)S(1)}, u32[]{:S(2)}, u32[]{:S(2)}) collective-permute-start(bf16[64,512]{1,0:T(8,128)(2,1)} %get-tuple-element.36), channel_id=1, source_target_pairs={{0,124},{4,0},{8,4},{12,8},{16,12},{20,16},{24,20},{28,24},{32,28}... | collective-permute-start | bytes 196616 | tf_op jit(solution)/shard_map/ppermute | solution.py:9
  78.4 91.8 %collective-permute-start.5 = (bf16[64,512]{1,0:T(8,128)(2,1)S(1)}, bf16[64,512]{1,0:T(8,128)(2,1)S(1)}, u32[]{:S(2)}, u32[]{:S(2)}) collective-permute-start(bf16[64,512]{1,0:T(8,128)(2,1)S(1)} %get-tuple-element.39), channel_id=1, source_target_pairs={{0,4},{4,8},{8,12},{12,16},{16,20},{20,24},{24,28},{28,32},{32,36}... | collective-permute-start | bytes 196616 | tf_op jit(solution)/shard_map/ppermute | solution.py:9
  78.4 91.8 %collective-permute-start.6 = (bf16[64,512]{1,0:T(8,128)(2,1)S(1)}, bf16[64,512]{1,0:T(8,128)(2,1)S(1)}, u32[]{:S(2)}, u32[]{:S(2)}) collective-permute-start(bf16[64,512]{1,0:T(8,128)(2,1)S(1)} %get-tuple-element.38), channel_id=1, source_target_pairs={{1,0},{2,1},{3,2},{5,4},{6,5},{7,6},{9,8},{10,9},{11,10},{13,12},{... | collective-permute-start | bytes 196616 | tf_op jit(solution)/shard_map/ppermute | solution.py:15
  79.7 90.6 %collective-permute-start.7 = (bf16[64,512]{1,0:T(8,128)(2,1)S(1)}, bf16[64,512]{1,0:T(8,128)(2,1)}, u32[]{:S(2)}, u32[]{:S(2)}) collective-permute-start(bf16[64,512]{1,0:T(8,128)(2,1)S(1)} %get-tuple-element.37), channel_id=1, source_target_pairs={{0,1},{1,2},{2,3},{4,5},{5,6},{6,7},{8,9},{9,10},{10,11},{12,13},{... | collective-permute-start | bytes 196616 | tf_op jit(solution)/shard_map/ppermute | solution.py:15
  95.8 9.0 %copy-start.11 = (f32[512]{0:T(512)S(1)}, f32[512]{0:T(512)}, u32[]{:S(2)}) copy-start(f32[512]{0:T(512)} %get-tuple-element.34) | copy-start | bytes 6148
  95.8 75.3 %copy-start.9 = (s32[256]{0:T(256)S(1)}, s32[256]{0:T(256)}, u32[]{:S(2)}) copy-start(s32[256]{0:T(256)} %copy-done.8) | copy-start | bytes 3076
  100.8 4.0 %copy-start.12 = (f32[512]{0:T(512)S(1)}, f32[512]{0:T(512)}, u32[]{:S(2)}) copy-start(f32[512]{0:T(512)} %get-tuple-element.26) | copy-start | bytes 6148
  100.8 4.0 %copy-start.13 = (f32[512]{0:T(512)S(1)}, f32[512]{0:T(512)}, u32[]{:S(2)}) copy-start(f32[512]{0:T(512)} %get-tuple-element.49) | copy-start | bytes 6148
  215.9 4.0 %copy-start.6 = (f32[512,512]{1,0:T(8,128)S(1)}, f32[512,512]{1,0:T(8,128)}, u32[]{:S(2)}) copy-start(f32[512,512]{1,0:T(8,128)} %get-tuple-element.61) | copy-start | bytes 3145732
  (5 other events, 8.7 us)
Sparse Core Ops, SparseCore 0:
  57.7 158.1 all-reduce.3
where the time goes:
time: 228 us
  blocking collectives  65.4 us (29%)
  matrix products  44.4 us (19%)
  waiting for transfers between devices  43.7 us (19%)
  local copies, waits for them, and re-layouts  30.6 us (13%)
  starting transfers between devices  19.2 us (8%)
  between operations  15.2 us (7%)
  other arithmetic  9.2 us (4%)
    psum x1, blocking collectives, body(): lax.psum((sums[0], sums[1], sums[2], sums[3], sums[4]), ('lon', 'lat'))  65.4 us
    psum x1, waiting for transfers between devices, body(): lax.psum((sums[0], sums[1], sums[2], sums[3], sums[4]), ('lon', 'lat'))  43.7 us
    unnamed x46, local copies, waits for them, and re-layouts  26.3 us
    ppermute x4, starting transfers between devices, passed_along_2(): lax.ppermute(value, axis, [(source, source + steps) for source in range(l...  11.2 us
    dot_general x2, matrix products, add_by_table(): lax.dot_general(onehot.astype(jnp.float32), values, (((0,), (0,)), ((), (...  9.05 us
    dot_general x1, matrix products, edge_backward(): lax.dot_general(joined, d_pre_b, (((0,), (0,)), ((), ())), preferred_elem...  8.78 us
    ppermute x4, starting transfers between devices, passed_along(): lax.ppermute(value, axis, [(i, (i + by) % size) for i in range(size)])  7.86 us
    dot_general x3, matrix products, pick_by_table(): jnp.dot(onehot, values, preferred_element_type=jnp.float32)  6.26 us
  transfers between devices with their start and end apart: 9, of which 1 were waited for; matrix products, arithmetic and copies ran while one was open for 20% of the time, Pallas kernels for 0%

commit v1 on v0

v1 whole, which is shorter than its diff:
```python
import functools

import jax
import jax.numpy as jnp
from jax import lax
from jax.experimental import pallas as pl
from jax.experimental.pallas import tpu as pltpu
from jax.sharding import PartitionSpec as P

F32, BF16 = jnp.float32, jnp.bfloat16
MESH = pl.DeviceIdType.MESH
D = 512
NODE = 256
EDGE = 2048
HALO = 64
EXT = NODE + 4 * HALO
TABLE = EXT + NODE
HALF = D // 2
QUARTER = HALF // 4
SIXTEENTH = QUARTER // 4
BLOCK = 128
CHUNK = 256
OUT, EDGES_IN, SENDERS_IN, RECEIVERS_IN = range(4)
AXES = (("x", "y", "z"), ("y", "z", "x"), ("z", "x", "y"), ("x", "z", "y"))


def dot(a, b, contract=(1, 0)):
    dims = (((contract[0],), (contract[1],)), ((), ()))
    return lax.dot_general(a, b, dims, preferred_element_type=F32)


def where_am_i():
    lon, lat = lax.axis_index("lon"), lax.axis_index("lat")
    return lon, lat, lon % 2, (lon // 2) % 4, lon // 8


class Place:
    def __init__(self):
        self.lon, self.lat, self.core, self.y, self.z = where_am_i()
        self.at = {"x": self.lat, "y": self.y, "z": self.z}
        self.partner = (self.lon + 1 - 2 * self.core, self.lat)
        self.east = ((self.lon + 1) % 32, self.lat)
        self.west = ((self.lon + 31) % 32, self.lat)
        self.north = (self.lon, (self.lat + 1) % 4)
        self.south = (self.lon, (self.lat + 3) % 4)
        self.beyond = ((self.lon + 31 + 2 * self.core) % 32, self.lat)

    def other(self, axis, step):
        spot = (self.at[axis] + step) % 4
        if axis == "x":
            return spot, (self.lon, spot)
        if axis == "y":
            return spot, (self.z * 8 + spot * 2 + self.core, self.lat)
        return spot, (spot * 8 + self.y * 2 + self.core, self.lat)


def remote(src, dst, send, recv, device):
    return pltpu.make_async_remote_copy(
        src_ref=src, dst_ref=dst, send_sem=send, recv_sem=recv, device_id=device, device_id_type=MESH
    )


def rows_at(start, size, unit):
    return pl.ds(pl.multiple_of(start, unit), size)


def kernel(
    comm,
    node_hbm, edge_hbm, sender, receiver, count, lists, w_in_hbm, b_in, w_out_hbm, b_out, gain, cot_hbm, ncot_hbm,
    edge_grad_hbm, node_grad, summed, vectors,
    ext, edge, cot, w_in, w_out, ncot, load_sem, store_sem,
    rows, slots, back_out, back, halo_send, halo_recv,
    onehot, onehot_t, list_t, proj, pre0, act, slope, d_mix, d_pre, q, own_table,
    grads, half_out, half_in, s1, r1, h2, s2, r2, h3, s3, r3, m_send, m_recv,
    v_core, v_axes, v_send, v_recv,
):
    me = Place()
    n_chunks = EDGE // CHUNK

    node_in = pltpu.make_async_copy(node_hbm, ext.at[pl.ds(0, NODE)], load_sem.at[0])
    w_in_in = pltpu.make_async_copy(w_in_hbm, w_in, load_sem.at[1])
    edge_in = pltpu.make_async_copy(edge_hbm, edge, load_sem.at[2])
    ncot_in = pltpu.make_async_copy(ncot_hbm, ncot, load_sem.at[3])
    w_out_in = pltpu.make_async_copy(w_out_hbm, w_out, load_sem.at[4])
    cot_in = pltpu.make_async_copy(cot_hbm, cot, load_sem.at[5])
    for copy in (node_in, w_in_in, edge_in, ncot_in, w_out_in, cot_in):
        copy.start()

    if comm:
        barrier = pltpu.get_barrier_semaphore()
        peers = [me.partner, me.beyond] + [me.other(axis, k)[1] for axis in "xyz" for k in (1, 2, 3)]
        for peer in peers:
            pl.semaphore_signal(barrier, inc=1, device_id=peer, device_id_type=MESH)

    list_row = jnp.concatenate([lists[0, k : k + 1, :] for k in range(4)], axis=1)
    in_list = lax.broadcasted_iota(jnp.int32, (NODE, 4 * HALO), 0) == list_row
    list_t[...] = jnp.where(in_list, 1.0, 0.0).astype(BF16)
    node_in.wait()
    rows[...] = dot(list_t[...], ext[:NODE], (0, 0)).astype(BF16)
    halo_to = (me.east, me.west, me.north, me.south)
    halo_copies = [
        remote(rows.at[pl.ds(k * HALO, HALO)], slots.at[pl.ds(k * HALO, HALO)], halo_send.at[k], halo_recv.at[k], halo_to[k])
        for k in range(4)
    ]
    if comm:
        pl.semaphore_wait(barrier, len(peers))
        for copy in halo_copies:
            copy.start()
    else:
        slots[...] = rows[...]

    def tables(j, _):
        here = rows_at(j * BLOCK, BLOCK, BLOCK)
        for index, first, width in ((sender, 0, EXT), (receiver, EXT, NODE)):
            row = index[pl.ds(j, 1), :]
            wide = jnp.broadcast_to(row, (BLOCK, BLOCK))
            column = wide.T
            for k in range(width // BLOCK):
                lane = lax.broadcasted_iota(jnp.int32, (BLOCK, BLOCK), 1) + k * BLOCK
                line = lax.broadcasted_iota(jnp.int32, (BLOCK, BLOCK), 0) + k * BLOCK
                spot = pl.ds(first + k * BLOCK, BLOCK)
                onehot[here, spot] = jnp.where(column == lane, 1.0, 0.0).astype(BF16)
                onehot_t[spot, here] = jnp.where(line == wide, 1.0, 0.0).astype(BF16)
        return 0

    lax.fori_loop(0, EDGE // BLOCK, tables, 0)

    w_in_in.wait()
    proj[:NODE] = dot(ext[:NODE], w_in[D : 2 * D]).astype(BF16)
    proj[EXT:] = dot(ext[:NODE], w_in[2 * D :]).astype(BF16)

    edge_in.wait()

    def first_layer(c, _):
        here = rows_at(c * CHUNK, CHUNK, CHUNK)
        pre0[here] = dot(edge[here], w_in[:D]) + b_in[...]
        return 0

    lax.fori_loop(0, n_chunks, first_layer, 0)

    if comm:
        for copy in halo_copies:
            copy.wait_recv()
    inside = (None, None, (me.lat > 0).astype(BF16), (me.lat < 3).astype(BF16))
    for k in range(4):
        block = slots[k * HALO : (k + 1) * HALO]
        ext[NODE + k * HALO : NODE + (k + 1) * HALO] = block if inside[k] is None else block * inside[k]
    proj[NODE:EXT] = dot(ext[NODE:], w_in[D : 2 * D]).astype(BF16)

    ncot_in.wait()
    w_out_in.wait()
    cot_in.wait()

    def through(c, sums):
        sum_gain, sum_out, sum_in = sums
        here = rows_at(c * CHUNK, CHUNK, CHUNK)
        pre = pre0[here] + dot(onehot[here, :], proj[...])
        sig = 0.5 * jnp.tanh(0.5 * pre) + 0.5
        act_b = (pre * sig).astype(BF16)
        act[here] = act_b
        slope[...] = sig * (1.0 + pre * (1.0 - sig))
        mixed = dot(act_b, w_out[...]) + b_out[...]
        centred = mixed - jnp.mean(mixed, axis=1, keepdims=True)
        scale = lax.rsqrt(jnp.mean(centred * centred, axis=1, keepdims=True) + 1e-05)
        normed = centred * scale
        live = lax.broadcasted_iota(jnp.int32, (CHUNK, 1), 0) + c * CHUNK < count[0]
        at_node = dot(onehot[here, EXT:], ncot[...])
        upstream = jnp.where(live, cot[here].astype(F32) + at_node, 0.0)
        both = upstream * normed
        scaled = upstream * gain[...]
        mean_s = jnp.mean(scaled, axis=1, keepdims=True)
        mean_sn = jnp.mean(both * gain[...], axis=1, keepdims=True)
        d_mixed = scale * (scaled - mean_s - normed * mean_sn)
        d_mixed_b = d_mixed.astype(BF16)
        d_mix[here] = d_mixed_b
        d_p = dot(d_mixed_b, w_out[...], (1, 1)) * slope[...]
        d_pre[here] = d_p.astype(BF16)
        fold = lambda a: jnp.sum(a.reshape(CHUNK // 8, 8, D), axis=0)
        return sum_gain + fold(both), sum_out + fold(d_mixed), sum_in + fold(d_p)

    zero = jnp.zeros((8, D), F32)
    sum_gain, sum_out, sum_in = lax.fori_loop(0, n_chunks, through, (zero, zero, zero))

    line = lax.broadcasted_iota(jnp.int32, (8, D), 0)
    total = jnp.zeros((8, D), F32)
    for k, part in enumerate((sum_in, sum_out, sum_gain)):
        total = jnp.where(line == k, jnp.sum(part, axis=0, keepdims=True), total)
    started = []

    def start(copy):
        copy.start()
        started.append(copy)

    v_copies = {}

    def vector_send(stage):
        if stage == "core":
            copies = [remote(v_core.at[me.core], v_core.at[me.core], v_send.at[0], v_recv.at[0], me.partner)]
        else:
            n = "xyz".index(stage)
            spot = me.at[stage]
            copies = [
                remote(
                    v_axes.at[n, spot], v_axes.at[n, spot],
                    v_send.at[1 + 3 * n + k - 1], v_recv.at[1 + 3 * n + k - 1], me.other(stage, k)[1],
                )
                for k in (1, 2, 3)
            ]
        for copy in copies:
            start(copy)
        v_copies[stage] = copies

    def vector_sum(stage):
        for copy in v_copies[stage]:
            copy.wait_recv()
        if stage == "core":
            return v_core[0] + v_core[1]
        n = "xyz".index(stage)
        return (v_axes[n, 0] + v_axes[n, 1]) + (v_axes[n, 2] + v_axes[n, 3])

    if comm:
        v_core[me.core] = total
        vector_send("core")
    else:
        vectors[...] = total

    m_copies = {}

    def matrix_send(m, stage, copies):
        for copy in copies:
            start(copy)
        m_copies[m, stage] = copies

    def matrix_wait(m, stage):
        for copy in m_copies[m, stage]:
            copy.wait_recv()

    def sems(m, stage, k=1):
        n = 0 if stage == 0 else 1 + 3 * (stage - 1) + k - 1
        return m_send.at[m, n], m_recv.at[m, n]

    mine = me.core * HALF
    theirs = HALF - mine

    def gradient(m, compute):
        first = compute(pl.multiple_of(theirs, HALF))
        if comm:
            half_out[m] = first.astype(BF16)
            matrix_send(m, 0, [remote(half_out.at[m], half_in.at[m], *sems(m, 0), me.partner)])
        grads[m] = compute(pl.multiple_of(mine, HALF))
        if not comm:
            summed[m * D : m * D + HALF] = first.astype(BF16)
            summed[m * D + HALF : (m + 1) * D] = grads[m].astype(BF16)

    def stage_1(m):
        matrix_wait(m, 0)
        grads[m] = grads[m] + half_in[m].astype(F32)
        s1[m] = grads[m].astype(BF16)
        copies = []
        for k in (1, 2, 3):
            spot, device = me.other(AXES[m][0], k)
            copies.append(remote(s1.at[m, rows_at(spot * QUARTER, QUARTER, QUARTER)], r1.at[m, k - 1], *sems(m, 1, k), device))
        matrix_send(m, 1, copies)

    def stage_2(m):
        matrix_wait(m, 1)
        spot = me.at[AXES[m][0]]
        part = grads[m, rows_at(spot * QUARTER, QUARTER, QUARTER)]
        for k in range(3):
            part = part + r1[m, k].astype(F32)
        h2[m] = part
        s2[m] = part.astype(BF16)
        copies = []
        for k in (1, 2, 3):
            spot, device = me.other(AXES[m][1], k)
            copies.append(remote(s2.at[m, rows_at(spot * SIXTEENTH, SIXTEENTH, SIXTEENTH)], r2.at[m, k - 1], *sems(m, 2, k), device))
        matrix_send(m, 2, copies)

    def stage_3(m):
        matrix_wait(m, 2)
        spot = me.at[AXES[m][1]]
        part = h2[m, rows_at(spot * SIXTEENTH, SIXTEENTH, SIXTEENTH)]
        for k in range(3):
            part = part + r2[m, k].astype(F32)
        h3[m] = part
        s3[m] = part.astype(BF16)
        copies = []
        for k in (1, 2, 3):
            spot, device = me.other(AXES[m][2], k)
            copies.append(remote(s3.at[m, :, rows_at(spot * BLOCK, BLOCK, BLOCK)], r3.at[m, k - 1], *sems(m, 3, k), device))
        matrix_send(m, 3, copies)

    def line_of(m, depth):
        begin = m * D + mine
        if depth >= 1:
            begin = begin + me.at[AXES[m][0]] * QUARTER
        if depth >= 2:
            begin = begin + me.at[AXES[m][1]] * SIXTEENTH
        return rows_at(begin, (HALF, QUARTER, SIXTEENTH)[depth], SIXTEENTH)

    def stage_4(m):
        matrix_wait(m, 3)
        lane = rows_at(me.at[AXES[m][2]] * BLOCK, BLOCK, BLOCK)
        part = h3[m, :, lane]
        for k in range(3):
            part = part + r3[m, k].astype(F32)
        summed[line_of(m, 2), lane] = part.astype(BF16)
        block = summed.at[line_of(m, 2), lane]
        matrix_send(m, 4, [remote(block, block, *sems(m, 4, k), me.other(AXES[m][2], k)[1]) for k in (1, 2, 3)])

    def stage_5(m):
        matrix_wait(m, 4)
        block = summed.at[line_of(m, 2)]
        matrix_send(m, 5, [remote(block, block, *sems(m, 5, k), me.other(AXES[m][1], k)[1]) for k in (1, 2, 3)])

    def stage_6(m):
        matrix_wait(m, 5)
        block = summed.at[line_of(m, 1)]
        matrix_send(m, 6, [remote(block, block, *sems(m, 6, k), me.other(AXES[m][0], k)[1]) for k in (1, 2, 3)])

    def stage_7(m):
        matrix_wait(m, 6)
        block = summed.at[line_of(m, 0)]
        matrix_send(m, 7, [remote(block, block, *sems(m, 7), me.partner)])

    def stage_8(m):
        matrix_wait(m, 7)

    gradient(OUT, lambda at: dot(act[:, pl.ds(at, HALF)], d_mix[...], (0, 0)))
    gradient(EDGES_IN, lambda at: dot(edge[:, pl.ds(at, HALF)], d_pre[...], (0, 0)))
    if comm:
        stage_1(OUT)
    q[...] = dot(onehot_t[...], d_pre[...]).astype(BF16)
    if comm:
        stage_1(EDGES_IN)
    gradient(SENDERS_IN, lambda at: dot(ext[:, pl.ds(at, HALF)], q[:EXT], (0, 0)))
    gradient(RECEIVERS_IN, lambda at: dot(ext[:NODE, pl.ds(at, HALF)], q[EXT:], (0, 0)))
    back_out[...] = dot(q[NODE:EXT], w_in[D : 2 * D], (1, 1)).astype(BF16)
    back_to = (me.west, me.east, me.south, me.north)
    back_copies = [
        remote(back_out.at[pl.ds(k * HALO, HALO)], back.at[pl.ds(k * HALO, HALO)], halo_send.at[4 + k], halo_recv.at[4 + k], back_to[k])
        for k in range(4)
    ]
    if comm:
        for copy in back_copies:
            start(copy)
        stage_2(OUT)
        stage_1(SENDERS_IN)
        stage_1(RECEIVERS_IN)
        v_axes[0, me.lat] = vector_sum("core")
        vector_send("x")
        stage_2(EDGES_IN)
        stage_3(OUT)
    else:
        back[...] = back_out[...]

    own_table[...] = dot(q[:NODE], w_in[D : 2 * D], (1, 1)) + dot(q[EXT:], w_in[2 * D :], (1, 1))

    def last(c, _):
        here = rows_at(c * CHUNK, CHUNK, CHUNK)
        live = lax.broadcasted_iota(jnp.int32, (CHUNK, 1), 0) + c * CHUNK < count[0]
        d_edge = dot(d_pre[here], w_in[:D], (1, 1))
        act[here] = jnp.where(live, cot[here].astype(F32) + d_edge, 0.0).astype(BF16)
        return 0

    lax.fori_loop(0, n_chunks, last, 0)
    edge_grad_out = pltpu.make_async_copy(act, edge_grad_hbm, store_sem.at[0])
    edge_grad_out.start()

    if comm:
        stage_2(SENDERS_IN)
        stage_2(RECEIVERS_IN)
        stage_3(EDGES_IN)
        stage_4(OUT)
        v_axes[1, me.y] = vector_sum("x")
        vector_send("y")
        for copy in back_copies:
            copy.wait_recv()
    back_in = (None, None, (me.lat < 3).astype(BF16), (me.lat > 0).astype(BF16))
    for k in range(4):
        if back_in[k] is not None:
            back[k * HALO : (k + 1) * HALO] = back[k * HALO : (k + 1) * HALO] * back_in[k]
    node_grad[...] = (own_table[...] + dot(list_t[...], back[...])).astype(BF16)

    if comm:
        stage_3(SENDERS_IN)
        stage_3(RECEIVERS_IN)
        stage_4(EDGES_IN)
        stage_5(OUT)
        v_axes[2, me.z] = vector_sum("y")
        vector_send("z")
        stage_4(SENDERS_IN)
        stage_4(RECEIVERS_IN)
        stage_5(EDGES_IN)
        stage_6(OUT)
        vectors[...] = vector_sum("z")
        stage_5(SENDERS_IN)
        stage_5(RECEIVERS_IN)
        stage_6(EDGES_IN)
        stage_7(OUT)
        stage_6(SENDERS_IN)
        stage_6(RECEIVERS_IN)
        stage_7(EDGES_IN)
        stage_7(SENDERS_IN)
        stage_7(RECEIVERS_IN)
        for m in range(4):
            stage_8(m)
        for copy in halo_copies + started:
            copy.wait_send()
    edge_grad_out.wait()


def call(comm, *args):
    vmem = pl.BlockSpec(memory_space=pltpu.VMEM)
    hbm = pl.BlockSpec(memory_space=pl.ANY)
    smem = pl.BlockSpec(memory_space=pltpu.SMEM)
    V = pltpu.VMEM
    dma = pltpu.SemaphoreType.DMA
    return pl.pallas_call(
        functools.partial(kernel, comm),
        out_shape=(
            jax.ShapeDtypeStruct((EDGE, D), BF16),
            jax.ShapeDtypeStruct((NODE, D), BF16),
            jax.ShapeDtypeStruct((4 * D, D), BF16),
            jax.ShapeDtypeStruct((8, D), F32),
        ),
        in_specs=[hbm, hbm, vmem, vmem, smem, vmem, hbm, vmem, hbm, vmem, vmem, hbm, hbm],
        out_specs=(hbm, vmem, vmem, vmem),
        scratch_shapes=[
            V((EXT, D), BF16), V((EDGE, D), BF16), V((EDGE, D), BF16), V((3 * D, D), BF16), V((D, D), BF16),
            V((NODE, D), BF16), dma((6,)), dma((1,)),
            V((4 * HALO, D), BF16), V((4 * HALO, D), BF16), V((4 * HALO, D), BF16), V((4 * HALO, D), BF16),
            dma((8,)), dma((8,)),
            V((EDGE, TABLE), BF16), V((TABLE, EDGE), BF16), V((NODE, 4 * HALO), BF16), V((TABLE, D), BF16),
            V((EDGE, D), F32), V((EDGE, D), BF16), V((CHUNK, D), F32), V((EDGE, D), BF16), V((EDGE, D), BF16),
            V((TABLE, D), BF16), V((NODE, D), F32),
            V((4, HALF, D), F32), V((4, HALF, D), BF16), V((4, HALF, D), BF16), V((4, HALF, D), BF16),
            V((4, 3, QUARTER, D), BF16), V((4, QUARTER, D), F32), V((4, QUARTER, D), BF16),
            V((4, 3, SIXTEENTH, D), BF16), V((4, SIXTEENTH, D), F32), V((4, SIXTEENTH, D), BF16),
            V((4, 3, SIXTEENTH, BLOCK), BF16), dma((4, 22)), dma((4, 22)),
            V((2, 8, D), F32), V((3, 4, 8, D), F32), dma((10,)), dma((10,)),
        ],
        compiler_params=pltpu.CompilerParams(
            collective_id=0 if comm else None, has_side_effects=True, vmem_limit_bytes=56 * 2**20
        ),
    )(*args)


def body(
    node_latent, edge_latent, edge_sender, edge_receiver, edge_count, halo_send,
    weight_in, bias_in, weight_out, bias_out, norm_gain, edge_cotangent, node_cotangent, comm=True,
):
    edge_grad, node_grad, summed, vectors = call(
        comm,
        node_latent, edge_latent, edge_sender.reshape(EDGE // BLOCK, BLOCK), edge_receiver.reshape(EDGE // BLOCK, BLOCK),
        edge_count, halo_send, weight_in, bias_in.reshape(1, D), weight_out, bias_out.reshape(1, D),
        norm_gain.reshape(1, D), edge_cotangent, node_cotangent,
    )
    summed = summed.astype(F32)
    return edge_grad, node_grad, summed[D:], vectors[0], summed[:D], vectors[1], vectors[2]


def solution(mesh):
    both = P(("lon", "lat"))
    rows = P(("lon", "lat"), None)
    return jax.shard_map(
        body,
        mesh=mesh,
        in_specs=(rows, rows, both, both, both, P(("lon", "lat"), None, None), P(), P(), P(), P(), P(), rows, rows),
        out_specs=(rows, rows, P(), P(), P(), P(), P()),
        check_vma=False,
    )
```

time: 228 us -> 72.6 us (0.32)
  blocking collectives: 65.4 us -> 0 us
  Pallas kernels: 0 us -> 63.3 us
  matrix products: 44.4 us -> 0 us
  waiting for transfers between devices: 43.7 us -> 0 us
  local copies, waits for them, and re-layouts: 30.6 us -> 7.77 us
  starting transfers between devices: 19.2 us -> 0 us
  between operations: 15.2 us -> 1.3 us
  other arithmetic: 9.2 us -> 0 us
    psum x1 -> x0, blocking collectives: 65.4 us -> none  [body(): lax.psum((sums[0], sums[1], sums[2], sums[3], sums[4]), ('lon', 'lat'))]
    pallas_call x0 -> x1, Pallas kernels: none -> 63.3 us  [call(): pl.pallas_call(functools.partial(kernel, comm), out_shape=(jax.ShapeDtype...]
    dot_general x13 -> x0, matrix products: 44.4 us -> none  [the longest x2 9.05 us: add_by_table(): lax.dot_general(onehot.astype(jnp.float32), values, (((0,), (0,)), ((), (...]
    psum x1 -> x0, waiting for transfers between devices: 43.7 us -> none  [body(): lax.psum((sums[0], sums[1], sums[2], sums[3], sums[4]), ('lon', 'lat'))]
    unnamed x46 -> x8, local copies, waits for them, and re-layouts: 26.3 us -> 2.03 us
    ppermute x8 -> x0, starting transfers between devices: 19.1 us -> none  [the longest x4 11.2 us: passed_along_2(): lax.ppermute(value, axis, [(source, source + steps) for source in range(l...]
    convert_element_type x2 -> x0, other arithmetic: 5.1 us -> none  [the longest x1 5.09 us: edge_backward(): (live * (edge_cot.astype(jnp.float32) + d_joined[:, :width])).astype(jnp....]
    reduce_sum x2 -> x0, other arithmetic: 3.18 us -> none  [the longest x1 2.56 us: edge_backward(): grad_b_out = jnp.sum(d_mixed, axis=0)]
  transfers between devices with their start and end apart: 9 -> 0, of which waited for: 1 -> 0; matrix products, arithmetic and copies ran while one was open for 20% -> 0% of each run, Pallas kernels for 0% -> 0%
where the time goes in v1:
time: 72.6 us; the launch traced here: 72.4 us
  Pallas kernels  63.3 us (87%)
  local copies, waits for them, and re-layouts  7.77 us (11%)
  between operations  1.3 us (2%)
    pallas_call x1, Pallas kernels, call(): pl.pallas_call(functools.partial(kernel, comm), out_shape=(jax.ShapeDtype...  63.3 us
    slice x1, local copies, waits for them, and re-layouts, body(): summed[:D]  2.14 us
    slice x1, local copies, waits for them, and re-layouts, body(): summed[D:]  2.1 us
    unnamed x8, local copies, waits for them, and re-layouts  2.03 us
    slice x1, local copies, waits for them, and re-layouts, body(): vectors[2]  1.49 us

profile of v1, /device:TPU:1, one launch (start us, length us, event | category | flops | bytes accessed | tf_op | source)
XLA Modules:
  0.0 72.4 jit_solution(8626487896522141579)
XLA Ops:
  1.3 63.3 %shard_map.180 = (bf16[2048,512]{1,0:T(8,128)(2,1)}, bf16[256,512]{1,0:T(8,128)(2,1)}, bf16[2048,512]{1,0:T(8,128)(2,1)}, f32[8,512]{1,0:T(8,128)}) custom-call(bf16[256,512]{1,0:T(8,128)(2,1)} %node_hbm.1, bf16[2048,512]{1,0:T(8,128)(2,1)} %edge_hbm.1, s32[16,128]{1,0:T(8,128)} %bitcast.8, s32[16,128]{1,0:T(8,128)} %bitcast.9, s32[1]{0:T(128)S(6)} %copy.22.count, ...), custom_call_target="tpu_custom_call" | custom-call | tf_op jit(solution)/shard_map/pallas_call | solution.py:419
  64.6 0.0 copy-start
  64.6 1.5 %fusion = (f32[1,512]{1,0:T(1,128)}, f32[1,512]{1,0:T(1,128)}, f32[1,512]{1,0:T(1,128)}) fusion(f32[8,512]{1,0:T(8,128)} %get-tuple-element.14), kind=kLoop, calls=%fused_computation | loop fusion | bytes 12288 | tf_op jit(solution)/shard_map/slice | solution.py:460
  66.1 2.1 %slice.21 = f32[512,512]{1,0:T(8,128)} slice(bf16[2048,512]{1,0:T(8,128)(2,1)} %get-tuple-element.13), slice={[0:512], [0:512]} | slice | bytes 2097152 | tf_op jit(solution)/shard_map/slice | solution.py:460
  68.2 0.0 copy-done
  68.2 0.0 copy-start.1
  68.2 2.1 %slice.20 = f32[1536,512]{1,0:T(8,128)} slice(bf16[2048,512]{1,0:T(8,128)(2,1)S(1)} %copy-done), slice={[512:2048], [0:512]} | slice | bytes 6291456 | tf_op jit(solution)/shard_map/slice | solution.py:460
  70.3 0.0 copy-done.1
  70.3 0.0 copy-start.2
  70.4 1.3 %copy.23 = bf16[2048,512]{1,0:T(8,128)(2,1)} copy(bf16[2048,512]{1,0:T(8,128)(2,1)S(1)} %copy-done.1) | data formatting | bytes 4194304
  71.7 0.0 copy-done.2
  71.7 0.7 copy.24
Async XLA Ops:
  64.6 3.6 %copy-start = (bf16[2048,512]{1,0:T(8,128)(2,1)S(1)}, bf16[2048,512]{1,0:T(8,128)(2,1)}, u32[]{:S(2)}) copy-start(bf16[2048,512]{1,0:T(8,128)(2,1)} %get-tuple-element.13) | copy-start | bytes 6291460
  68.2 2.1 %copy-start.1 = (bf16[2048,512]{1,0:T(8,128)(2,1)S(1)}, bf16[2048,512]{1,0:T(8,128)(2,1)}, u32[]{:S(2)}) copy-start(bf16[2048,512]{1,0:T(8,128)(2,1)} %get-tuple-element.25) | copy-start | bytes 6291460
  70.3 1.3 %copy-start.2 = (bf16[256,512]{1,0:T(8,128)(2,1)S(1)}, bf16[256,512]{1,0:T(8,128)(2,1)}, u32[]{:S(2)}) copy-start(bf16[256,512]{1,0:T(8,128)(2,1)} %get-tuple-element.26) | copy-start | bytes 786436

commit v2 on v1

--- a/solution.py
+++ b/solution.py
@@ -22,6 +22,8 @@
 CHUNK = 256
 OUT, EDGES_IN, SENDERS_IN, RECEIVERS_IN = range(4)
 AXES = (("x", "y", "z"), ("y", "z", "x"), ("z", "x", "y"), ("x", "z", "y"))
+PLANE = [(i, j) for i in range(4) for j in range(4) if (i, j) != (0, 0)]
+PLANE.sort(key=lambda step: -(min(step[0], 4 - step[0]) + min(step[1], 4 - step[1])))
 
 
 def dot(a, b, contract=(1, 0)):
@@ -47,11 +49,18 @@
 
     def other(self, axis, step):
         spot = (self.at[axis] + step) % 4
-        if axis == "x":
-            return spot, (self.lon, spot)
-        if axis == "y":
-            return spot, (self.z * 8 + spot * 2 + self.core, self.lat)
-        return spot, (spot * 8 + self.y * 2 + self.core, self.lat)
+        return spot, self.device({axis: spot})
+
+    def device(self, spots):
+        at = {**self.at, **spots}
+        return (at["z"] * 8 + at["y"] * 2 + self.core, at["x"])
+
+    def plane(self, axes):
+        found = []
+        for step in PLANE:
+            spots = [(self.at[axis] + by) % 4 for axis, by in zip(axes, step)]
+            found.append((*spots, self.device(dict(zip(axes, spots)))))
+        return found
 
 
 def remote(src, dst, send, recv, device):
@@ -67,12 +76,12 @@
 def kernel(
     comm,
     node_hbm, edge_hbm, sender, receiver, count, lists, w_in_hbm, b_in, w_out_hbm, b_out, gain, cot_hbm, ncot_hbm,
-    edge_grad_hbm, node_grad, summed, vectors,
-    ext, edge, cot, w_in, w_out, ncot, load_sem, store_sem,
+    edge_grad, node_grad, sum_out, sum_in, vectors,
+    ext, edge, cot, w_in, w_out, ncot, load_sem,
     rows, slots, back_out, back, halo_send, halo_recv,
     onehot, onehot_t, list_t, proj, pre0, act, slope, d_mix, d_pre, q, own_table,
-    grads, half_out, half_in, s1, r1, h2, s2, r2, h3, s3, r3, m_send, m_recv,
-    v_core, v_axes, v_send, v_recv,
+    grads, half_out, half_in, s1, r1, h2, s2, r2, m_send, m_recv,
+    v_core, v_axes, v_send, v_recv, plane_sem,
 ):
     me = Place()
     n_chunks = EDGE // CHUNK
@@ -106,6 +115,8 @@
         pl.semaphore_wait(barrier, len(peers))
         for copy in halo_copies:
             copy.start()
+        for peer in peers[2:]:
+            pl.semaphore_signal(plane_sem, inc=1, device_id=peer, device_id_type=MESH)
     else:
         slots[...] = rows[...]
 
@@ -152,7 +163,7 @@
     cot_in.wait()
 
     def through(c, sums):
-        sum_gain, sum_out, sum_in = sums
+        gain_rows, out_rows, in_rows = sums
         here = rows_at(c * CHUNK, CHUNK, CHUNK)
         pre = pre0[here] + dot(onehot[here, :], proj[...])
         sig = 0.5 * jnp.tanh(0.5 * pre) + 0.5
@@ -176,14 +187,14 @@
         d_p = dot(d_mixed_b, w_out[...], (1, 1)) * slope[...]
         d_pre[here] = d_p.astype(BF16)
         fold = lambda a: jnp.sum(a.reshape(CHUNK // 8, 8, D), axis=0)
-        return sum_gain + fold(both), sum_out + fold(d_mixed), sum_in + fold(d_p)
+        return gain_rows + fold(both), out_rows + fold(d_mixed), in_rows + fold(d_p)
 
     zero = jnp.zeros((8, D), F32)
-    sum_gain, sum_out, sum_in = lax.fori_loop(0, n_chunks, through, (zero, zero, zero))
+    gain_rows, out_rows, in_rows = lax.fori_loop(0, n_chunks, through, (zero, zero, zero))
 
     line = lax.broadcasted_iota(jnp.int32, (8, D), 0)
     total = jnp.zeros((8, D), F32)
-    for k, part in enumerate((sum_in, sum_out, sum_gain)):
+    for k, part in enumerate((in_rows, out_rows, gain_rows)):
         total = jnp.where(line == k, jnp.sum(part, axis=0, keepdims=True), total)
     started = []
 
@@ -235,8 +246,8 @@
         for copy in m_copies[m, stage]:
             copy.wait_recv()
 
-    def sems(m, stage, k=1):
-        n = 0 if stage == 0 else 1 + 3 * (stage - 1) + k - 1
+    def sems(m, stage, k=0):
+        n = (0, 1, 4, 19, 34, 37)[stage] + k
         return m_send.at[m, n], m_recv.at[m, n]
 
     mine = me.core * HALF
@@ -249,17 +260,18 @@
             matrix_send(m, 0, [remote(half_out.at[m], half_in.at[m], *sems(m, 0), me.partner)])
         grads[m] = compute(pl.multiple_of(mine, HALF))
         if not comm:
-            summed[m * D : m * D + HALF] = first.astype(BF16)
-            summed[m * D + HALF : (m + 1) * D] = grads[m].astype(BF16)
+            sum_out[:HALF] = first.astype(BF16)
+            sum_out[HALF:] = grads[m].astype(BF16)
+            sum_in[0] = sum_out[...]
 
     def stage_1(m):
         matrix_wait(m, 0)
         grads[m] = grads[m] + half_in[m].astype(F32)
         s1[m] = grads[m].astype(BF16)
         copies = []
-        for k in (1, 2, 3):
-            spot, device = me.other(AXES[m][0], k)
-            copies.append(remote(s1.at[m, rows_at(spot * QUARTER, QUARTER, QUARTER)], r1.at[m, k - 1], *sems(m, 1, k), device))
+        for k in range(3):
+            spot, device = me.other(AXES[m][0], (2, 1, 3)[k])
+            copies.append(remote(s1.at[m, rows_at(spot * QUARTER, QUARTER, QUARTER)], r1.at[m, k], *sems(m, 1, k), device))
         matrix_send(m, 1, copies)
 
     def stage_2(m):
@@ -271,68 +283,52 @@
         h2[m] = part
         s2[m] = part.astype(BF16)
         copies = []
-        for k in (1, 2, 3):
-            spot, device = me.other(AXES[m][1], k)
-            copies.append(remote(s2.at[m, rows_at(spot * SIXTEENTH, SIXTEENTH, SIXTEENTH)], r2.at[m, k - 1], *sems(m, 2, k), device))
+        for k, (line, lane, device) in enumerate(me.plane(AXES[m][1:])):
+            piece = s2.at[m, rows_at(line * SIXTEENTH, SIXTEENTH, SIXTEENTH), rows_at(lane * BLOCK, BLOCK, BLOCK)]
+            copies.append(remote(piece, r2.at[m, k], *sems(m, 2, k), device))
         matrix_send(m, 2, copies)
 
-    def stage_3(m):
-        matrix_wait(m, 2)
-        spot = me.at[AXES[m][1]]
-        part = h2[m, rows_at(spot * SIXTEENTH, SIXTEENTH, SIXTEENTH)]
-        for k in range(3):
-            part = part + r2[m, k].astype(F32)
-        h3[m] = part
-        s3[m] = part.astype(BF16)
-        copies = []
-        for k in (1, 2, 3):
-            spot, device = me.other(AXES[m][2], k)
-            copies.append(remote(s3.at[m, :, rows_at(spot * BLOCK, BLOCK, BLOCK)], r3.at[m, k - 1], *sems(m, 3, k), device))
-        matrix_send(m, 3, copies)
-
-    def line_of(m, depth):
-        begin = m * D + mine
+    def block_of(m, depth):
+        begin = mine
         if depth >= 1:
             begin = begin + me.at[AXES[m][0]] * QUARTER
         if depth >= 2:
             begin = begin + me.at[AXES[m][1]] * SIXTEENTH
-        return rows_at(begin, (HALF, QUARTER, SIXTEENTH)[depth], SIXTEENTH)
+        line = rows_at(begin, (HALF, QUARTER, SIXTEENTH)[depth], SIXTEENTH)
+        if m == OUT:
+            return sum_out.at[line]
+        return sum_in.at[m - 1, line]
+
+    def stage_3(m):
+        matrix_wait(m, 2)
+        lane = rows_at(me.at[AXES[m][2]] * BLOCK, BLOCK, BLOCK)
+        part = h2[m, rows_at(me.at[AXES[m][1]] * SIXTEENTH, SIXTEENTH, SIXTEENTH), lane]
+        for k in range(15):
+            part = part + r2[m, k].astype(F32)
+        block = block_of(m, 2).at[:, lane]
+        block[...] = part.astype(BF16)
+        peers = me.plane(AXES[m][1:])
+        matrix_send(m, 3, [remote(block, block, *sems(m, 3, k), peers[k][2]) for k in range(15)])
 
     def stage_4(m):
         matrix_wait(m, 3)
-        lane = rows_at(me.at[AXES[m][2]] * BLOCK, BLOCK, BLOCK)
-        part = h3[m, :, lane]
-        for k in range(3):
-            part = part + r3[m, k].astype(F32)
-        summed[line_of(m, 2), lane] = part.astype(BF16)
-        block = summed.at[line_of(m, 2), lane]
-        matrix_send(m, 4, [remote(block, block, *sems(m, 4, k), me.other(AXES[m][2], k)[1]) for k in (1, 2, 3)])
+        block = block_of(m, 1)
+        matrix_send(m, 4, [remote(block, block, *sems(m, 4, k), me.other(AXES[m][0], (2, 1, 3)[k])[1]) for k in range(3)])
 
     def stage_5(m):
         matrix_wait(m, 4)
-        block = summed.at[line_of(m, 2)]
-        matrix_send(m, 5, [remote(block, block, *sems(m, 5, k), me.other(AXES[m][1], k)[1]) for k in (1, 2, 3)])
+        block = block_of(m, 0)
+        matrix_send(m, 5, [remote(block, block, *sems(m, 5), me.partner)])
 
     def stage_6(m):
         matrix_wait(m, 5)
-        block = summed.at[line_of(m, 1)]
-        matrix_send(m, 6, [remote(block, block, *sems(m, 6, k), me.other(AXES[m][0], k)[1]) for k in (1, 2, 3)])
-
-    def stage_7(m):
-        matrix_wait(m, 6)
-        block = summed.at[line_of(m, 0)]
-        matrix_send(m, 7, [remote(block, block, *sems(m, 7), me.partner)])
-
-    def stage_8(m):
-        matrix_wait(m, 7)
-
+
+    if comm:
+        pl.semaphore_wait(plane_sem, 9)
     gradient(OUT, lambda at: dot(act[:, pl.ds(at, HALF)], d_mix[...], (0, 0)))
-    gradient(EDGES_IN, lambda at: dot(edge[:, pl.ds(at, HALF)], d_pre[...], (0, 0)))
+    q[...] = dot(onehot_t[...], d_pre[...]).astype(BF16)
     if comm:
         stage_1(OUT)
-    q[...] = dot(onehot_t[...], d_pre[...]).astype(BF16)
-    if comm:
-        stage_1(EDGES_IN)
     gradient(SENDERS_IN, lambda at: dot(ext[:, pl.ds(at, HALF)], q[:EXT], (0, 0)))
     gradient(RECEIVERS_IN, lambda at: dot(ext[:NODE, pl.ds(at, HALF)], q[EXT:], (0, 0)))
     back_out[...] = dot(q[NODE:EXT], w_in[D : 2 * D], (1, 1)).astype(BF16)
@@ -344,34 +340,34 @@
     if comm:
         for copy in back_copies:
             start(copy)
-        stage_2(OUT)
         stage_1(SENDERS_IN)
         stage_1(RECEIVERS_IN)
+    else:
+        back[...] = back_out[...]
+    gradient(EDGES_IN, lambda at: dot(edge[:, pl.ds(at, HALF)], d_pre[...], (0, 0)))
+    if comm:
+        stage_2(OUT)
         v_axes[0, me.lat] = vector_sum("core")
         vector_send("x")
-        stage_2(EDGES_IN)
-        stage_3(OUT)
-    else:
-        back[...] = back_out[...]
 
     own_table[...] = dot(q[:NODE], w_in[D : 2 * D], (1, 1)) + dot(q[EXT:], w_in[2 * D :], (1, 1))
+    if comm:
+        stage_1(EDGES_IN)
 
     def last(c, _):
         here = rows_at(c * CHUNK, CHUNK, CHUNK)
         live = lax.broadcasted_iota(jnp.int32, (CHUNK, 1), 0) + c * CHUNK < count[0]
         d_edge = dot(d_pre[here], w_in[:D], (1, 1))
-        act[here] = jnp.where(live, cot[here].astype(F32) + d_edge, 0.0).astype(BF16)
+        edge_grad[here] = jnp.where(live, cot[here].astype(F32) + d_edge, 0.0).astype(BF16)
         return 0
 
     lax.fori_loop(0, n_chunks, last, 0)
-    edge_grad_out = pltpu.make_async_copy(act, edge_grad_hbm, store_sem.at[0])
-    edge_grad_out.start()
 
     if comm:
         stage_2(SENDERS_IN)
         stage_2(RECEIVERS_IN)
-        stage_3(EDGES_IN)
-        stage_4(OUT)
+        stage_2(EDGES_IN)
+        stage_3(OUT)
         v_axes[1, me.y] = vector_sum("x")
         vector_send("y")
         for copy in back_copies:
@@ -385,50 +381,40 @@
     if comm:
         stage_3(SENDERS_IN)
         stage_3(RECEIVERS_IN)
-        stage_4(EDGES_IN)
-        stage_5(OUT)
+        stage_3(EDGES_IN)
+        stage_4(OUT)
         v_axes[2, me.z] = vector_sum("y")
         vector_send("z")
         stage_4(SENDERS_IN)
         stage_4(RECEIVERS_IN)
-        stage_5(EDGES_IN)
-        stage_6(OUT)
+        stage_4(EDGES_IN)
+        stage_5(OUT)
         vectors[...] = vector_sum("z")
         stage_5(SENDERS_IN)
         stage_5(RECEIVERS_IN)
-        stage_6(EDGES_IN)
-        stage_7(OUT)
-        stage_6(SENDERS_IN)
-        stage_6(RECEIVERS_IN)
-        stage_7(EDGES_IN)
-        stage_7(SENDERS_IN)
-        stage_7(RECEIVERS_IN)
+        stage_5(EDGES_IN)
         for m in range(4):
-            stage_8(m)
+            stage_6(m)
         for copy in halo_copies + started:
             copy.wait_send()
-    edge_grad_out.wait()
 
 
 def call(comm, *args):
     vmem = pl.BlockSpec(memory_space=pltpu.VMEM)
-    hbm = pl.BlockSpec(memory_space=pl.ANY)
+    hbm = pl.BlockSpec(memory_space=pltpu.HBM)
     smem = pl.BlockSpec(memory_space=pltpu.SMEM)
     V = pltpu.VMEM
     dma = pltpu.SemaphoreType.DMA
     return pl.pallas_call(
         functools.partial(kernel, comm),
         out_shape=(
-            jax.ShapeDtypeStruct((EDGE, D), BF16),
-            jax.ShapeDtypeStruct((NODE, D), BF16),
-            jax.ShapeDtypeStruct((4 * D, D), BF16),
-            jax.ShapeDtypeStruct((8, D), F32),
+            V((EDGE, D), BF16), V((NODE, D), BF16), V((D, D), BF16), V((3, D, D), BF16), V((8, D), F32),
         ),
         in_specs=[hbm, hbm, vmem, vmem, smem, vmem, hbm, vmem, hbm, vmem, vmem, hbm, hbm],
-        out_specs=(hbm, vmem, vmem, vmem),
+        out_specs=(vmem, vmem, vmem, vmem, vmem),
         scratch_shapes=[
             V((EXT, D), BF16), V((EDGE, D), BF16), V((EDGE, D), BF16), V((3 * D, D), BF16), V((D, D), BF16),
-            V((NODE, D), BF16), dma((6,)), dma((1,)),
+            V((NODE, D), BF16), dma((6,)),
             V((4 * HALO, D), BF16), V((4 * HALO, D), BF16), V((4 * HALO, D), BF16), V((4 * HALO, D), BF16),
             dma((8,)), dma((8,)),
             V((EDGE, TABLE), BF16), V((TABLE, EDGE), BF16), V((NODE, 4 * HALO), BF16), V((TABLE, D), BF16),
@@ -436,13 +422,51 @@
             V((TABLE, D), BF16), V((NODE, D), F32),
             V((4, HALF, D), F32), V((4, HALF, D), BF16), V((4, HALF, D), BF16), V((4, HALF, D), BF16),
             V((4, 3, QUARTER, D), BF16), V((4, QUARTER, D), F32), V((4, QUARTER, D), BF16),
-            V((4, 3, SIXTEENTH, D), BF16), V((4, SIXTEENTH, D), F32), V((4, SIXTEENTH, D), BF16),
-            V((4, 3, SIXTEENTH, BLOCK), BF16), dma((4, 22)), dma((4, 22)),
-            V((2, 8, D), F32), V((3, 4, 8, D), F32), dma((10,)), dma((10,)),
+            V((4, 15, SIXTEENTH, BLOCK), BF16), dma((4, 38)), dma((4, 38)),
+            V((2, 8, D), F32), V((3, 4, 8, D), F32), dma((10,)), dma((10,)), pltpu.SemaphoreType.REGULAR,
         ],
         compiler_params=pltpu.CompilerParams(
-            collective_id=0 if comm else None, has_side_effects=True, vmem_limit_bytes=56 * 2**20
+            collective_id=0 if comm else None, has_side_effects=True, vmem_limit_bytes=57 * 2**20
         ),
+    )(*args)
+
+
+def finish_kernel(
+    edge_grad, node_grad, sum_out, sum_in, vectors,
+    edge_grad_hbm, node_grad_hbm, w_in_hbm, b_in_out, w_out_hbm, b_out_out, gain_out,
+    wide, sem,
+):
+    copies = [
+        pltpu.make_async_copy(edge_grad, edge_grad_hbm, sem.at[0]),
+        pltpu.make_async_copy(node_grad, node_grad_hbm, sem.at[1]),
+    ]
+    for copy in copies:
+        copy.start()
+    for m in range(4):
+        wide[m] = (sum_in[m] if m < 3 else sum_out[...]).astype(F32)
+        to = w_in_hbm.at[pl.ds(m * D, D)] if m < 3 else w_out_hbm
+        copies.append(pltpu.make_async_copy(wide.at[m], to, sem.at[2 + m]))
+        copies[-1].start()
+    for k, out in enumerate((b_in_out, b_out_out, gain_out)):
+        out[...] = vectors[k : k + 1, :]
+    for copy in copies:
+        copy.wait()
+
+
+def finish(*args):
+    vmem = pl.BlockSpec(memory_space=pltpu.VMEM)
+    hbm = pl.BlockSpec(memory_space=pltpu.HBM)
+    vector = jax.ShapeDtypeStruct((1, D), F32)
+    return pl.pallas_call(
+        finish_kernel,
+        out_shape=(
+            jax.ShapeDtypeStruct((EDGE, D), BF16), jax.ShapeDtypeStruct((NODE, D), BF16),
+            jax.ShapeDtypeStruct((3 * D, D), F32), vector, jax.ShapeDtypeStruct((D, D), F32), vector, vector,
+        ),
+        in_specs=[vmem] * 5,
+        out_specs=(hbm, hbm, hbm, vmem, hbm, vmem, vmem),
+        scratch_shapes=[pltpu.VMEM((4, D, D), F32), pltpu.SemaphoreType.DMA((6,))],
+        compiler_params=pltpu.CompilerParams(vmem_limit_bytes=12 * 2**20),
     )(*args)
 
 
@@ -450,14 +474,14 @@
     node_latent, edge_latent, edge_sender, edge_receiver, edge_count, halo_send,
     weight_in, bias_in, weight_out, bias_out, norm_gain, edge_cotangent, node_cotangent, comm=True,
 ):
-    edge_grad, node_grad, summed, vectors = call(
+    results = call(
         comm,
         node_latent, edge_latent, edge_sender.reshape(EDGE // BLOCK, BLOCK), edge_receiver.reshape(EDGE // BLOCK, BLOCK),
         edge_count, halo_send, weight_in, bias_in.reshape(1, D), weight_out, bias_out.reshape(1, D),
         norm_gain.reshape(1, D), edge_cotangent, node_cotangent,
     )
-    summed = summed.astype(F32)
-    return edge_grad, node_grad, summed[D:], vectors[0], summed[:D], vectors[1], vectors[2]
+    edge_grad, node_grad, w_in, b_in, w_out, b_out, gain = finish(*results)
+    return edge_grad, node_grad, w_in, b_in.reshape(D), w_out, b_out.reshape(D), gain.reshape(D)
 
 
 def solution(mesh):

time: 72.6 us -> 61.6 us (0.85)
  local copies, waits for them, and re-layouts: 7.77 us -> 0 us
  Pallas kernels: 63.3 us -> 60.1 us
    slice x3 -> x0, local copies, waits for them, and re-layouts: 5.74 us -> none  [the longest x1 2.14 us: body(): summed[:D]]
    pallas_call x1 -> x2, Pallas kernels: 63.3 us -> 60.1 us  [the longest x1 56.7 us: call(): pl.pallas_call(functools.partial(kernel, comm), out_shape=(V((EDGE, D), B...]
    unnamed x8 -> x0, local copies, waits for them, and re-layouts: 2.03 us -> none
where the time goes in v2:
time: 61.6 us; the launch traced here: 61.4 us
  Pallas kernels  60.1 us (98%)
  between operations  1.29 us (2%)
    pallas_call x1, Pallas kernels, call(): pl.pallas_call(functools.partial(kernel, comm), out_shape=(V((EDGE, D), B...  56.7 us
    pallas_call x1, Pallas kernels, finish(): pl.pallas_call(finish_kernel, out_shape=(jax.ShapeDtypeStruct((EDGE, D),...  3.39 us

profile of v2, /device:TPU:1, one launch (start us, length us, event | category | flops | bytes accessed | tf_op | source)
XLA Modules:
  0.0 61.4 jit_solution(14948382736944881886)
XLA Ops:
  1.3 56.7 %shard_map.180 = (bf16[2048,512]{1,0:T(8,128)(2,1)S(1)}, bf16[256,512]{1,0:T(8,128)(2,1)S(1)}, bf16[512,512]{1,0:T(8,128)(2,1)S(1)}, bf16[3,512,512]{2,1,0:T(8,128)(2,1)S(1)}, f32[8,512]{1,0:T(8,128)S(1)}) custom-call(bf16[256,512]{1,0:T(8,128)(2,1)} %node_hbm.1, bf16[2048,512]{1,0:T(8,128)(2,1)} %edge_hbm.1, s32[16,128]{1,0:T(8,128)} %bitcast.8, ...), custom_call_target="tpu_custom_call" | custom-call | tf_op jit(solution)/shard_map/pallas_call | solution.py:408
  58.0 3.4 %shard_map.181 = (bf16[2048,512]{1,0:T(8,128)(2,1)}, bf16[256,512]{1,0:T(8,128)(2,1)}, f32[1536,512]{1,0:T(8,128)}, f32[1,512]{1,0:T(1,128)}, f32[512,512]{1,0:T...) custom-call(bf16[2048,512]{1,0:T(8,128)(2,1)S(1)} %get-tuple-element.19.edge_grad, ...), custom_call_target="tpu_custom_call" | custom-call | tf_op jit(solution)/shard_map/pallas_call | solution.py:460

commit v3 on v2

--- a/solution.py
+++ b/solution.py
@@ -19,7 +19,9 @@
 QUARTER = HALF // 4
 SIXTEENTH = QUARTER // 4
 BLOCK = 128
-CHUNK = 256
+CHUNK = 1024
+SUB = 32
+UNROLL = True
 OUT, EDGES_IN, SENDERS_IN, RECEIVERS_IN = range(4)
 AXES = (("x", "y", "z"), ("y", "z", "x"), ("z", "x", "y"), ("x", "z", "y"))
 PLANE = [(i, j) for i in range(4) for j in range(4) if (i, j) != (0, 0)]
@@ -75,36 +77,39 @@
 
 def kernel(
     comm,
-    node_hbm, edge_hbm, sender, receiver, count, lists, w_in_hbm, b_in, w_out_hbm, b_out, gain, cot_hbm, ncot_hbm,
+    node_hbm, edge_hbm, sender_hbm, receiver_hbm, count, lists_hbm, w_in_hbm, b_in_hbm, w_out_hbm, b_out_hbm, gain_hbm, cot_hbm, ncot_hbm,
     edge_grad, node_grad, sum_out, sum_in, vectors,
-    ext, edge, cot, w_in, w_out, ncot, load_sem,
+    lists, sender, receiver, b_in, b_out, gain, ext, edge, cot, w_in, w_out, ncot, load_sem,
     rows, slots, back_out, back, halo_send, halo_recv,
-    onehot, onehot_t, list_t, proj, pre0, act, slope, d_mix, d_pre, q, own_table,
+    onehot, onehot_t, list_t, proj, pre0, act, slope, half, mixed_s, at_node, d_mix, d_pre, q, own_table,
     grads, half_out, half_in, s1, r1, h2, s2, r2, m_send, m_recv,
     v_core, v_axes, v_send, v_recv, plane_sem,
 ):
     me = Place()
     n_chunks = EDGE // CHUNK
 
-    node_in = pltpu.make_async_copy(node_hbm, ext.at[pl.ds(0, NODE)], load_sem.at[0])
-    w_in_in = pltpu.make_async_copy(w_in_hbm, w_in, load_sem.at[1])
-    edge_in = pltpu.make_async_copy(edge_hbm, edge, load_sem.at[2])
-    ncot_in = pltpu.make_async_copy(ncot_hbm, ncot, load_sem.at[3])
-    w_out_in = pltpu.make_async_copy(w_out_hbm, w_out, load_sem.at[4])
-    cot_in = pltpu.make_async_copy(cot_hbm, cot, load_sem.at[5])
-    for copy in (node_in, w_in_in, edge_in, ncot_in, w_out_in, cot_in):
-        copy.start()
-
     if comm:
         barrier = pltpu.get_barrier_semaphore()
-        peers = [me.partner, me.beyond] + [me.other(axis, k)[1] for axis in "xyz" for k in (1, 2, 3)]
+        peers = [me.partner, me.beyond] + [me.other(axis, k)[1] for axis in "xyz" for k in (1, 3, 2)]
         for peer in peers:
             pl.semaphore_signal(barrier, inc=1, device_id=peer, device_id_type=MESH)
 
+    loads = [
+        pltpu.make_async_copy(src, dst, load_sem.at[n])
+        for n, (src, dst) in enumerate((
+            (lists_hbm, lists), (node_hbm, ext.at[pl.ds(0, NODE)]), (sender_hbm, sender), (receiver_hbm, receiver),
+            (w_in_hbm, w_in), (b_in_hbm, b_in), (edge_hbm, edge), (w_out_hbm, w_out), (ncot_hbm, ncot),
+            (b_out_hbm, b_out), (gain_hbm, gain), (cot_hbm, cot),
+        ))
+    ]
+    for copy in loads:
+        copy.start()
+
+    loads[0].wait()
     list_row = jnp.concatenate([lists[0, k : k + 1, :] for k in range(4)], axis=1)
     in_list = lax.broadcasted_iota(jnp.int32, (NODE, 4 * HALO), 0) == list_row
     list_t[...] = jnp.where(in_list, 1.0, 0.0).astype(BF16)
-    node_in.wait()
+    loads[1].wait()
     rows[...] = dot(list_t[...], ext[:NODE], (0, 0)).astype(BF16)
     halo_to = (me.east, me.west, me.north, me.south)
     halo_copies = [
@@ -134,17 +139,20 @@
                 onehot_t[spot, here] = jnp.where(line == wide, 1.0, 0.0).astype(BF16)
         return 0
 
+    loads[2].wait()
+    loads[3].wait()
     lax.fori_loop(0, EDGE // BLOCK, tables, 0)
 
-    w_in_in.wait()
-    proj[:NODE] = dot(ext[:NODE], w_in[D : 2 * D]).astype(BF16)
-    proj[EXT:] = dot(ext[:NODE], w_in[2 * D :]).astype(BF16)
-
-    edge_in.wait()
+    loads[4].wait()
+    proj[:NODE] = (0.5 * dot(ext[:NODE], w_in[D : 2 * D])).astype(BF16)
+    proj[EXT:] = (0.5 * dot(ext[:NODE], w_in[2 * D :])).astype(BF16)
+
+    loads[5].wait()
+    loads[6].wait()
 
     def first_layer(c, _):
         here = rows_at(c * CHUNK, CHUNK, CHUNK)
-        pre0[here] = dot(edge[here], w_in[:D]) + b_in[...]
+        pre0[here] = 0.5 * (dot(edge[here], w_in[:D]) + b_in[...])
         return 0
 
     lax.fori_loop(0, n_chunks, first_layer, 0)
@@ -156,46 +164,64 @@
     for k in range(4):
         block = slots[k * HALO : (k + 1) * HALO]
         ext[NODE + k * HALO : NODE + (k + 1) * HALO] = block if inside[k] is None else block * inside[k]
-    proj[NODE:EXT] = dot(ext[NODE:], w_in[D : 2 * D]).astype(BF16)
-
-    ncot_in.wait()
-    w_out_in.wait()
-    cot_in.wait()
+    proj[NODE:EXT] = (0.5 * dot(ext[NODE:], w_in[D : 2 * D])).astype(BF16)
+
+    for copy in loads[7:]:
+        copy.wait()
+
+    gain_row, b_out_row = gain[...], b_out[...]
+    fold = lambda a: jnp.sum(a.reshape(-1, 8, D), axis=0)
+    mean = lambda a: jnp.sum(a, axis=1, keepdims=True) * (1.0 / D)
 
     def through(c, sums):
         gain_rows, out_rows, in_rows = sums
-        here = rows_at(c * CHUNK, CHUNK, CHUNK)
-        pre = pre0[here] + dot(onehot[here, :], proj[...])
-        sig = 0.5 * jnp.tanh(0.5 * pre) + 0.5
-        act_b = (pre * sig).astype(BF16)
-        act[here] = act_b
-        slope[...] = sig * (1.0 + pre * (1.0 - sig))
-        mixed = dot(act_b, w_out[...]) + b_out[...]
-        centred = mixed - jnp.mean(mixed, axis=1, keepdims=True)
-        scale = lax.rsqrt(jnp.mean(centred * centred, axis=1, keepdims=True) + 1e-05)
-        normed = centred * scale
-        live = lax.broadcasted_iota(jnp.int32, (CHUNK, 1), 0) + c * CHUNK < count[0]
-        at_node = dot(onehot[here, EXT:], ncot[...])
-        upstream = jnp.where(live, cot[here].astype(F32) + at_node, 0.0)
-        both = upstream * normed
-        scaled = upstream * gain[...]
-        mean_s = jnp.mean(scaled, axis=1, keepdims=True)
-        mean_sn = jnp.mean(both * gain[...], axis=1, keepdims=True)
-        d_mixed = scale * (scaled - mean_s - normed * mean_sn)
-        d_mixed_b = d_mixed.astype(BF16)
-        d_mix[here] = d_mixed_b
-        d_p = dot(d_mixed_b, w_out[...], (1, 1)) * slope[...]
-        d_pre[here] = d_p.astype(BF16)
-        fold = lambda a: jnp.sum(a.reshape(CHUNK // 8, 8, D), axis=0)
-        return gain_rows + fold(both), out_rows + fold(d_mixed), in_rows + fold(d_p)
+        start = c * CHUNK
+        here = rows_at(start, CHUNK, CHUNK)
+        buf = c % 2 if isinstance(c, int) else 0
+        half[buf] = pre0[here] + dot(onehot[here, :], proj[...])
+        for r in range(0, CHUNK, SUB):
+            there = rows_at(start + r, SUB, SUB)
+            h = half[buf, r : r + SUB]
+            u = 1.0 + jnp.tanh(h)
+            a = h * u
+            act[there] = a.astype(BF16)
+            slope[buf, r : r + SUB] = a + (0.5 * u) * (1.0 - a)
+        mixed_s[buf] = dot(act[here], w_out[...])
+        at_node[buf] = dot(onehot[here, EXT:], ncot[...])
+        for r in range(0, CHUNK, SUB):
+            there = rows_at(start + r, SUB, SUB)
+            mixed = mixed_s[buf, r : r + SUB] + b_out_row
+            centred = mixed - mean(mixed)
+            live = lax.broadcasted_iota(jnp.int32, (SUB, 1), 0) + (start + r) < count[0]
+            scale = jnp.where(live, lax.rsqrt(mean(centred * centred) + 1e-05), 0.0)
+            normed = centred * scale
+            scaled = (cot[there].astype(F32) + at_node[buf, r : r + SUB]) * gain_row
+            both = scaled * normed
+            d_mixed = scaled * scale - mean(scaled) * scale - normed * (mean(both) * scale)
+            d_mix[there] = d_mixed.astype(BF16)
+            gain_rows, out_rows = gain_rows + fold(both), out_rows + fold(d_mixed)
+        half[buf] = dot(d_mix[here], w_out[...], (1, 1))
+        for r in range(0, CHUNK, SUB):
+            there = rows_at(start + r, SUB, SUB)
+            d_p = half[buf, r : r + SUB] * slope[buf, r : r + SUB]
+            d_pre[there] = d_p.astype(BF16)
+            in_rows = in_rows + fold(d_p)
+        return gain_rows, out_rows, in_rows
 
     zero = jnp.zeros((8, D), F32)
-    gain_rows, out_rows, in_rows = lax.fori_loop(0, n_chunks, through, (zero, zero, zero))
+    sums = (zero, zero, zero)
+    if UNROLL:
+        for c in range(n_chunks):
+            sums = through(c, sums)
+    else:
+        sums = lax.fori_loop(0, n_chunks, through, sums)
+    gain_rows, out_rows, in_rows = sums
 
     line = lax.broadcasted_iota(jnp.int32, (8, D), 0)
     total = jnp.zeros((8, D), F32)
     for k, part in enumerate((in_rows, out_rows, gain_rows)):
-        total = jnp.where(line == k, jnp.sum(part, axis=0, keepdims=True), total)
+        part = jnp.sum(part, axis=0, keepdims=True)
+        total = jnp.where(line == k, part / gain_row if k == 2 else part, total)
     started = []
 
     def start(copy):
@@ -410,15 +436,18 @@
         out_shape=(
             V((EDGE, D), BF16), V((NODE, D), BF16), V((D, D), BF16), V((3, D, D), BF16), V((8, D), F32),
         ),
-        in_specs=[hbm, hbm, vmem, vmem, smem, vmem, hbm, vmem, hbm, vmem, vmem, hbm, hbm],
+        in_specs=[hbm] * 4 + [smem] + [hbm] * 8,
         out_specs=(vmem, vmem, vmem, vmem, vmem),
         scratch_shapes=[
+            V((1, 4, HALO), jnp.int32), V((EDGE // BLOCK, BLOCK), jnp.int32), V((EDGE // BLOCK, BLOCK), jnp.int32),
+            V((1, D), F32), V((1, D), F32), V((1, D), F32),
             V((EXT, D), BF16), V((EDGE, D), BF16), V((EDGE, D), BF16), V((3 * D, D), BF16), V((D, D), BF16),
-            V((NODE, D), BF16), dma((6,)),
+            V((NODE, D), BF16), dma((12,)),
             V((4 * HALO, D), BF16), V((4 * HALO, D), BF16), V((4 * HALO, D), BF16), V((4 * HALO, D), BF16),
             dma((8,)), dma((8,)),
             V((EDGE, TABLE), BF16), V((TABLE, EDGE), BF16), V((NODE, 4 * HALO), BF16), V((TABLE, D), BF16),
-            V((EDGE, D), F32), V((EDGE, D), BF16), V((CHUNK, D), F32), V((EDGE, D), BF16), V((EDGE, D), BF16),
+            V((EDGE, D), F32), V((EDGE, D), BF16), V((2, CHUNK, D), F32), V((2, CHUNK, D), F32), V((2, CHUNK, D), F32), V((2, CHUNK, D), F32),
+            V((EDGE, D), BF16), V((EDGE, D), BF16),
             V((TABLE, D), BF16), V((NODE, D), F32),
             V((4, HALF, D), F32), V((4, HALF, D), BF16), V((4, HALF, D), BF16), V((4, HALF, D), BF16),
             V((4, 3, QUARTER, D), BF16), V((4, QUARTER, D), F32), V((4, QUARTER, D), BF16),

time: 61.6 us -> 58 us (0.942)
  Pallas kernels: 60.1 us -> 56.4 us
    pallas_call x1, Pallas kernels: 56.7 us -> 53.1 us  [call(): pl.pallas_call(functools.partial(kernel, comm), out_shape=(V((EDGE, D), B...]
where the time goes in v3:
time: 58 us; the launch traced here: 57.9 us
  Pallas kernels  56.4 us (97%)
  between operations  1.45 us (2%)
    pallas_call x1, Pallas kernels, call(): pl.pallas_call(functools.partial(kernel, comm), out_shape=(V((EDGE, D), B...  53.1 us
    pallas_call x1, Pallas kernels, finish(): pl.pallas_call(finish_kernel, out_shape=(jax.ShapeDtypeStruct((EDGE, D),...  3.39 us

profile of v3, /device:TPU:1, one launch (start us, length us, event | category | flops | bytes accessed | tf_op | source)
XLA Modules:
  0.0 57.9 jit_solution(13974547413651565561)
XLA Ops:
  1.3 53.1 %shard_map.180 = (bf16[2048,512]{1,0:T(8,128)(2,1)S(1)}, bf16[256,512]{1,0:T(8,128)(2,1)S(1)}, bf16[512,512]{1,0:T(8,128)(2,1)S(1)}, bf16[3,512,512]{2,1,0:T(8,128)(2,1)S(1)}, f32[8,512]{1,0:T(8,128)S(1)}) custom-call(bf16[256,512]{1,0:T(8,128)(2,1)} %node_hbm.1, bf16[2048,512]{1,0:T(8,128)(2,1)} %edge_hbm.1, s32[16,128]{1,0:T(8,128)} %bitcast.8, ...), custom_call_target="tpu_custom_call" | custom-call | tf_op jit(solution)/shard_map/pallas_call | solution.py:434
  54.3 3.4 %shard_map.181 = (bf16[2048,512]{1,0:T(8,128)(2,1)}, bf16[256,512]{1,0:T(8,128)(2,1)}, f32[1536,512]{1,0:T(8,128)}, f32[1,512]{1,0:T(1,128)}, f32[512,512]{1,0:T...) custom-call(bf16[2048,512]{1,0:T(8,128)(2,1)S(1)} %get-tuple-element.19.edge_grad, ...), custom_call_target="tpu_custom_call" | custom-call | tf_op jit(solution)/shard_map/pallas_call | solution.py:489

commit v4 on v3

--- a/solution.py
+++ b/solution.py
@@ -22,7 +22,7 @@
 CHUNK = 1024
 SUB = 32
 UNROLL = True
-OUT, EDGES_IN, SENDERS_IN, RECEIVERS_IN = range(4)
+OUT, SENDERS_IN, RECEIVERS_IN, EDGES_IN = range(4)
 AXES = (("x", "y", "z"), ("y", "z", "x"), ("z", "x", "y"), ("x", "z", "y"))
 PLANE = [(i, j) for i in range(4) for j in range(4) if (i, j) != (0, 0)]
 PLANE.sort(key=lambda step: -(min(step[0], 4 - step[0]) + min(step[1], 4 - step[1])))
@@ -71,15 +71,19 @@
     )
 
 
+def arrived(like, sem):
+    pltpu.make_async_copy(like, like, sem).wait()
+
+
 def rows_at(start, size, unit):
     return pl.ds(pl.multiple_of(start, unit), size)
 
 
 def kernel(
     comm,
-    node_hbm, edge_hbm, sender_hbm, receiver_hbm, count, lists_hbm, w_in_hbm, b_in_hbm, w_out_hbm, b_out_hbm, gain_hbm, cot_hbm, ncot_hbm,
+    node_hbm, edge_hbm, sender_hbm, receiver_hbm, count_hbm, lists_hbm, w_in_hbm, b_in_hbm, w_out_hbm, b_out_hbm, gain_hbm, cot_hbm, ncot_hbm,
     edge_grad, node_grad, sum_out, sum_in, vectors,
-    lists, sender, receiver, b_in, b_out, gain, ext, edge, cot, w_in, w_out, ncot, load_sem,
+    count, lists, sender, receiver, b_in, b_out, gain, ext, edge, cot, w_in, w_out, ncot, load_sem,
     rows, slots, back_out, back, halo_send, halo_recv,
     onehot, onehot_t, list_t, proj, pre0, act, slope, half, mixed_s, at_node, d_mix, d_pre, q, own_table,
     grads, half_out, half_in, s1, r1, h2, s2, r2, m_send, m_recv,
@@ -99,7 +103,7 @@
         for n, (src, dst) in enumerate((
             (lists_hbm, lists), (node_hbm, ext.at[pl.ds(0, NODE)]), (sender_hbm, sender), (receiver_hbm, receiver),
             (w_in_hbm, w_in), (b_in_hbm, b_in), (edge_hbm, edge), (w_out_hbm, w_out), (ncot_hbm, ncot),
-            (b_out_hbm, b_out), (gain_hbm, gain), (cot_hbm, cot),
+            (b_out_hbm, b_out), (gain_hbm, gain), (count_hbm, count), (cot_hbm, cot),
         ))
     ]
     for copy in loads:
@@ -113,7 +117,7 @@
     rows[...] = dot(list_t[...], ext[:NODE], (0, 0)).astype(BF16)
     halo_to = (me.east, me.west, me.north, me.south)
     halo_copies = [
-        remote(rows.at[pl.ds(k * HALO, HALO)], slots.at[pl.ds(k * HALO, HALO)], halo_send.at[k], halo_recv.at[k], halo_to[k])
+        remote(rows.at[pl.ds(k * HALO, HALO)], slots.at[pl.ds(k * HALO, HALO)], halo_send.at[0], halo_recv.at[0], halo_to[k])
         for k in range(4)
     ]
     if comm:
@@ -158,8 +162,7 @@
     lax.fori_loop(0, n_chunks, first_layer, 0)
 
     if comm:
-        for copy in halo_copies:
-            copy.wait_recv()
+        arrived(slots, halo_recv.at[0])
     inside = (None, None, (me.lat > 0).astype(BF16), (me.lat < 3).astype(BF16))
     for k in range(4):
         block = slots[k * HALO : (k + 1) * HALO]
@@ -222,37 +225,21 @@
     for k, part in enumerate((in_rows, out_rows, gain_rows)):
         part = jnp.sum(part, axis=0, keepdims=True)
         total = jnp.where(line == k, part / gain_row if k == 2 else part, total)
-    started = []
-
-    def start(copy):
-        copy.start()
-        started.append(copy)
-
-    v_copies = {}
-
     def vector_send(stage):
         if stage == "core":
-            copies = [remote(v_core.at[me.core], v_core.at[me.core], v_send.at[0], v_recv.at[0], me.partner)]
+            remote(v_core.at[me.core], v_core.at[me.core], v_send.at[0], v_recv.at[0], me.partner).start()
         else:
             n = "xyz".index(stage)
-            spot = me.at[stage]
-            copies = [
-                remote(
-                    v_axes.at[n, spot], v_axes.at[n, spot],
-                    v_send.at[1 + 3 * n + k - 1], v_recv.at[1 + 3 * n + k - 1], me.other(stage, k)[1],
-                )
-                for k in (1, 2, 3)
-            ]
-        for copy in copies:
-            start(copy)
-        v_copies[stage] = copies
+            here = v_axes.at[n, me.at[stage]]
+            for k in (2, 1, 3):
+                remote(here, here, v_send.at[1 + n], v_recv.at[1 + n], me.other(stage, k)[1]).start()
 
     def vector_sum(stage):
-        for copy in v_copies[stage]:
-            copy.wait_recv()
         if stage == "core":
+            arrived(v_core.at[0], v_recv.at[0])
             return v_core[0] + v_core[1]
         n = "xyz".index(stage)
+        arrived(v_axes.at[n, pl.ds(0, 3)], v_recv.at[1 + n])
         return (v_axes[n, 0] + v_axes[n, 1]) + (v_axes[n, 2] + v_axes[n, 3])
 
     if comm:
@@ -261,20 +248,18 @@
     else:
         vectors[...] = total
 
-    m_copies = {}
-
     def matrix_send(m, stage, copies):
         for copy in copies:
-            start(copy)
-        m_copies[m, stage] = copies
+            copy.start()
 
     def matrix_wait(m, stage):
-        for copy in m_copies[m, stage]:
-            copy.wait_recv()
-
-    def sems(m, stage, k=0):
-        n = (0, 1, 4, 19, 34, 37)[stage] + k
-        return m_send.at[m, n], m_recv.at[m, n]
+        arrived(like(m, stage), m_recv.at[m, stage])
+
+    def sems(m, stage):
+        return m_send.at[m, stage], m_recv.at[m, stage]
+
+    def like(m, stage):
+        return (half_in, r1, r2, r2, r1, half_in)[stage].at[m]
 
     mine = me.core * HALF
     theirs = HALF - mine
@@ -297,7 +282,7 @@
         copies = []
         for k in range(3):
             spot, device = me.other(AXES[m][0], (2, 1, 3)[k])
-            copies.append(remote(s1.at[m, rows_at(spot * QUARTER, QUARTER, QUARTER)], r1.at[m, k], *sems(m, 1, k), device))
+            copies.append(remote(s1.at[m, rows_at(spot * QUARTER, QUARTER, QUARTER)], r1.at[m, k], *sems(m, 1), device))
         matrix_send(m, 1, copies)
 
     def stage_2(m):
@@ -311,7 +296,7 @@
         copies = []
         for k, (line, lane, device) in enumerate(me.plane(AXES[m][1:])):
             piece = s2.at[m, rows_at(line * SIXTEENTH, SIXTEENTH, SIXTEENTH), rows_at(lane * BLOCK, BLOCK, BLOCK)]
-            copies.append(remote(piece, r2.at[m, k], *sems(m, 2, k), device))
+            copies.append(remote(piece, r2.at[m, k], *sems(m, 2), device))
         matrix_send(m, 2, copies)
 
     def block_of(m, depth):
@@ -323,7 +308,7 @@
         line = rows_at(begin, (HALF, QUARTER, SIXTEENTH)[depth], SIXTEENTH)
         if m == OUT:
             return sum_out.at[line]
-        return sum_in.at[m - 1, line]
+        return sum_in.at[m % 3, line]
 
     def stage_3(m):
         matrix_wait(m, 2)
@@ -334,12 +319,12 @@
         block = block_of(m, 2).at[:, lane]
         block[...] = part.astype(BF16)
         peers = me.plane(AXES[m][1:])
-        matrix_send(m, 3, [remote(block, block, *sems(m, 3, k), peers[k][2]) for k in range(15)])
+        matrix_send(m, 3, [remote(block, block, *sems(m, 3), peers[k][2]) for k in range(15)])
 
     def stage_4(m):
         matrix_wait(m, 3)
         block = block_of(m, 1)
-        matrix_send(m, 4, [remote(block, block, *sems(m, 4, k), me.other(AXES[m][0], (2, 1, 3)[k])[1]) for k in range(3)])
+        matrix_send(m, 4, [remote(block, block, *sems(m, 4), me.other(AXES[m][0], (2, 1, 3)[k])[1]) for k in range(3)])
 
     def stage_5(m):
         matrix_wait(m, 4)
@@ -349,33 +334,28 @@
     def stage_6(m):
         matrix_wait(m, 5)
 
-    if comm:
-        pl.semaphore_wait(plane_sem, 9)
     gradient(OUT, lambda at: dot(act[:, pl.ds(at, HALF)], d_mix[...], (0, 0)))
     q[...] = dot(onehot_t[...], d_pre[...]).astype(BF16)
-    if comm:
-        stage_1(OUT)
     gradient(SENDERS_IN, lambda at: dot(ext[:, pl.ds(at, HALF)], q[:EXT], (0, 0)))
     gradient(RECEIVERS_IN, lambda at: dot(ext[:NODE, pl.ds(at, HALF)], q[EXT:], (0, 0)))
     back_out[...] = dot(q[NODE:EXT], w_in[D : 2 * D], (1, 1)).astype(BF16)
     back_to = (me.west, me.east, me.south, me.north)
     back_copies = [
-        remote(back_out.at[pl.ds(k * HALO, HALO)], back.at[pl.ds(k * HALO, HALO)], halo_send.at[4 + k], halo_recv.at[4 + k], back_to[k])
+        remote(back_out.at[pl.ds(k * HALO, HALO)], back.at[pl.ds(k * HALO, HALO)], halo_send.at[1], halo_recv.at[1], back_to[k])
         for k in range(4)
     ]
     if comm:
+        stage_1(OUT)
         for copy in back_copies:
-            start(copy)
-        stage_1(SENDERS_IN)
-        stage_1(RECEIVERS_IN)
+            copy.start()
     else:
         back[...] = back_out[...]
     gradient(EDGES_IN, lambda at: dot(edge[:, pl.ds(at, HALF)], d_pre[...], (0, 0)))
     if comm:
-        stage_2(OUT)
+        stage_1(SENDERS_IN)
+        stage_1(RECEIVERS_IN)
         v_axes[0, me.lat] = vector_sum("core")
         vector_send("x")
-
     own_table[...] = dot(q[:NODE], w_in[D : 2 * D], (1, 1)) + dot(q[EXT:], w_in[2 * D :], (1, 1))
     if comm:
         stage_1(EDGES_IN)
@@ -390,14 +370,12 @@
     lax.fori_loop(0, n_chunks, last, 0)
 
     if comm:
-        stage_2(SENDERS_IN)
-        stage_2(RECEIVERS_IN)
-        stage_2(EDGES_IN)
-        stage_3(OUT)
+        pl.semaphore_wait(plane_sem, 9)
+        for m in range(4):
+            stage_2(m)
         v_axes[1, me.y] = vector_sum("x")
         vector_send("y")
-        for copy in back_copies:
-            copy.wait_recv()
+        arrived(back, halo_recv.at[1])
     back_in = (None, None, (me.lat < 3).astype(BF16), (me.lat > 0).astype(BF16))
     for k in range(4):
         if back_in[k] is not None:
@@ -405,30 +383,30 @@
     node_grad[...] = (own_table[...] + dot(list_t[...], back[...])).astype(BF16)
 
     if comm:
-        stage_3(SENDERS_IN)
-        stage_3(RECEIVERS_IN)
-        stage_3(EDGES_IN)
-        stage_4(OUT)
+        for m in range(4):
+            stage_3(m)
         v_axes[2, me.z] = vector_sum("y")
         vector_send("z")
-        stage_4(SENDERS_IN)
-        stage_4(RECEIVERS_IN)
-        stage_4(EDGES_IN)
-        stage_5(OUT)
+        for m in range(4):
+            stage_4(m)
         vectors[...] = vector_sum("z")
-        stage_5(SENDERS_IN)
-        stage_5(RECEIVERS_IN)
-        stage_5(EDGES_IN)
+        for m in range(4):
+            stage_5(m)
         for m in range(4):
             stage_6(m)
-        for copy in halo_copies + started:
-            copy.wait_send()
+        arrived(rows, halo_send.at[0])
+        arrived(back_out, halo_send.at[1])
+        arrived(v_core.at[0], v_send.at[0])
+        for n in range(3):
+            arrived(v_axes.at[n, pl.ds(0, 3)], v_send.at[1 + n])
+        for m in range(4):
+            for stage in range(6):
+                arrived(like(m, stage), m_send.at[m, stage])
 
 
 def call(comm, *args):
     vmem = pl.BlockSpec(memory_space=pltpu.VMEM)
     hbm = pl.BlockSpec(memory_space=pltpu.HBM)
-    smem = pl.BlockSpec(memory_space=pltpu.SMEM)
     V = pltpu.VMEM
     dma = pltpu.SemaphoreType.DMA
     return pl.pallas_call(
@@ -436,23 +414,23 @@
         out_shape=(
             V((EDGE, D), BF16), V((NODE, D), BF16), V((D, D), BF16), V((3, D, D), BF16), V((8, D), F32),
         ),
-        in_specs=[hbm] * 4 + [smem] + [hbm] * 8,
+        in_specs=[hbm] * 13,
         out_specs=(vmem, vmem, vmem, vmem, vmem),
         scratch_shapes=[
-            V((1, 4, HALO), jnp.int32), V((EDGE // BLOCK, BLOCK), jnp.int32), V((EDGE // BLOCK, BLOCK), jnp.int32),
+            pltpu.SMEM((1,), jnp.int32), V((1, 4, HALO), jnp.int32), V((EDGE // BLOCK, BLOCK), jnp.int32), V((EDGE // BLOCK, BLOCK), jnp.int32),
             V((1, D), F32), V((1, D), F32), V((1, D), F32),
             V((EXT, D), BF16), V((EDGE, D), BF16), V((EDGE, D), BF16), V((3 * D, D), BF16), V((D, D), BF16),
-            V((NODE, D), BF16), dma((12,)),
+            V((NODE, D), BF16), dma((13,)),
             V((4 * HALO, D), BF16), V((4 * HALO, D), BF16), V((4 * HALO, D), BF16), V((4 * HALO, D), BF16),
-            dma((8,)), dma((8,)),
+            dma((2,)), dma((2,)),
             V((EDGE, TABLE), BF16), V((TABLE, EDGE), BF16), V((NODE, 4 * HALO), BF16), V((TABLE, D), BF16),
             V((EDGE, D), F32), V((EDGE, D), BF16), V((2, CHUNK, D), F32), V((2, CHUNK, D), F32), V((2, CHUNK, D), F32), V((2, CHUNK, D), F32),
             V((EDGE, D), BF16), V((EDGE, D), BF16),
             V((TABLE, D), BF16), V((NODE, D), F32),
             V((4, HALF, D), F32), V((4, HALF, D), BF16), V((4, HALF, D), BF16), V((4, HALF, D), BF16),
             V((4, 3, QUARTER, D), BF16), V((4, QUARTER, D), F32), V((4, QUARTER, D), BF16),
-            V((4, 15, SIXTEENTH, BLOCK), BF16), dma((4, 38)), dma((4, 38)),
-            V((2, 8, D), F32), V((3, 4, 8, D), F32), dma((10,)), dma((10,)), pltpu.SemaphoreType.REGULAR,
+            V((4, 15, SIXTEENTH, BLOCK), BF16), dma((4, 6)), dma((4, 6)),
+            V((2, 8, D), F32), V((3, 4, 8, D), F32), dma((4,)), dma((4,)), pltpu.SemaphoreType.REGULAR,
         ],
         compiler_params=pltpu.CompilerParams(
             collective_id=0 if comm else None, has_side_effects=True, vmem_limit_bytes=57 * 2**20

time: 58 us -> 54.1 us (0.933)
  Pallas kernels: 56.4 us -> 52.7 us
    pallas_call x1, Pallas kernels: 53.1 us -> 49.3 us  [call(): pl.pallas_call(functools.partial(kernel, comm), out_shape=(V((EDGE, D), B...]
where the time goes in v4:
time: 54.1 us; the launch traced here: 53.9 us
  Pallas kernels  52.7 us (97%)
  between operations  1.29 us (2%)
    pallas_call x1, Pallas kernels, call(): pl.pallas_call(functools.partial(kernel, comm), out_shape=(V((EDGE, D), B...  49.3 us
    pallas_call x1, Pallas kernels, finish(): pl.pallas_call(finish_kernel, out_shape=(jax.ShapeDtypeStruct((EDGE, D),...  3.39 us

profile of v4, /device:TPU:1, one launch (start us, length us, event | category | flops | bytes accessed | tf_op | source)
XLA Modules:
  0.0 53.9 jit_solution(7968908542686862781)
XLA Ops:
  1.3 49.3 %shard_map.180 = (bf16[2048,512]{1,0:T(8,128)(2,1)S(1)}, bf16[256,512]{1,0:T(8,128)(2,1)S(1)}, bf16[512,512]{1,0:T(8,128)(2,1)S(1)}, bf16[3,512,512]{2,1,0:T(8,128)(2,1)S(1)}, f32[8,512]{1,0:T(8,128)S(1)}) custom-call(bf16[256,512]{1,0:T(8,128)(2,1)} %node_hbm.1, bf16[2048,512]{1,0:T(8,128)(2,1)} %edge_hbm.1, s32[16,128]{1,0:T(8,128)} %bitcast.8, ...), custom_call_target="tpu_custom_call" | custom-call | tf_op jit(solution)/shard_map/pallas_call | solution.py:412
  50.6 3.4 %shard_map.181 = (bf16[2048,512]{1,0:T(8,128)(2,1)}, bf16[256,512]{1,0:T(8,128)(2,1)}, f32[1536,512]{1,0:T(8,128)}, f32[1,512]{1,0:T(1,128)}, f32[512,512]{1,0:T...) custom-call(bf16[2048,512]{1,0:T(8,128)(2,1)S(1)} %get-tuple-element.19.edge_grad, ...), custom_call_target="tpu_custom_call" | custom-call | tf_op jit(solution)/shard_map/pallas_call | solution.py:467

commit v5 on v4

--- a/solution.py
+++ b/solution.py
@@ -21,7 +21,6 @@
 BLOCK = 128
 CHUNK = 1024
 SUB = 32
-UNROLL = True
 OUT, SENDERS_IN, RECEIVERS_IN, EDGES_IN = range(4)
 AXES = (("x", "y", "z"), ("y", "z", "x"), ("z", "x", "y"), ("x", "z", "y"))
 PLANE = [(i, j) for i in range(4) for j in range(4) if (i, j) != (0, 0)]
@@ -85,7 +84,7 @@
     edge_grad, node_grad, sum_out, sum_in, vectors,
     count, lists, sender, receiver, b_in, b_out, gain, ext, edge, cot, w_in, w_out, ncot, load_sem,
     rows, slots, back_out, back, halo_send, halo_recv,
-    onehot, onehot_t, list_t, proj, pre0, act, slope, half, mixed_s, at_node, d_mix, d_pre, q, own_table,
+    onehot, onehot_t, list_t, proj, pre0, act, slope, half, mixed_s, at_node, acc_edge, acc_q, d_mix, d_pre, q, own_table,
     grads, half_out, half_in, s1, r1, h2, s2, r2, m_send, m_recv,
     v_core, v_axes, v_send, v_recv, plane_sem,
 ):
@@ -176,14 +175,13 @@
     fold = lambda a: jnp.sum(a.reshape(-1, 8, D), axis=0)
     mean = lambda a: jnp.sum(a, axis=1, keepdims=True) * (1.0 / D)
 
-    def through(c, sums):
-        gain_rows, out_rows, in_rows = sums
-        start = c * CHUNK
-        here = rows_at(start, CHUNK, CHUNK)
-        buf = c % 2 if isinstance(c, int) else 0
+    def forward(c, sums):
+        gain_rows, out_rows = sums
+        start, buf = c * CHUNK, c
+        here = pl.ds(start, CHUNK)
         half[buf] = pre0[here] + dot(onehot[here, :], proj[...])
         for r in range(0, CHUNK, SUB):
-            there = rows_at(start + r, SUB, SUB)
+            there = pl.ds(start + r, SUB)
             h = half[buf, r : r + SUB]
             u = 1.0 + jnp.tanh(h)
             a = h * u
@@ -192,7 +190,7 @@
         mixed_s[buf] = dot(act[here], w_out[...])
         at_node[buf] = dot(onehot[here, EXT:], ncot[...])
         for r in range(0, CHUNK, SUB):
-            there = rows_at(start + r, SUB, SUB)
+            there = pl.ds(start + r, SUB)
             mixed = mixed_s[buf, r : r + SUB] + b_out_row
             centred = mixed - mean(mixed)
             live = lax.broadcasted_iota(jnp.int32, (SUB, 1), 0) + (start + r) < count[0]
@@ -203,28 +201,25 @@
             d_mixed = scaled * scale - mean(scaled) * scale - normed * (mean(both) * scale)
             d_mix[there] = d_mixed.astype(BF16)
             gain_rows, out_rows = gain_rows + fold(both), out_rows + fold(d_mixed)
+        return gain_rows, out_rows
+
+    def backward(c, in_rows):
+        start, buf = c * CHUNK, c
+        here = pl.ds(start, CHUNK)
         half[buf] = dot(d_mix[here], w_out[...], (1, 1))
+        if c:
+            before = pl.ds(start - CHUNK, CHUNK)
+            new_edge = dot(edge[before], d_pre[before], (0, 0))
+            new_q = dot(onehot_t[:, before], d_pre[before])
+            acc_edge[...] = new_edge if c == 1 else acc_edge[...] + new_edge
+            acc_q[...] = new_q if c == 1 else acc_q[...] + new_q
         for r in range(0, CHUNK, SUB):
-            there = rows_at(start + r, SUB, SUB)
+            there = pl.ds(start + r, SUB)
             d_p = half[buf, r : r + SUB] * slope[buf, r : r + SUB]
             d_pre[there] = d_p.astype(BF16)
             in_rows = in_rows + fold(d_p)
-        return gain_rows, out_rows, in_rows
-
-    zero = jnp.zeros((8, D), F32)
-    sums = (zero, zero, zero)
-    if UNROLL:
-        for c in range(n_chunks):
-            sums = through(c, sums)
-    else:
-        sums = lax.fori_loop(0, n_chunks, through, sums)
-    gain_rows, out_rows, in_rows = sums
-
-    line = lax.broadcasted_iota(jnp.int32, (8, D), 0)
-    total = jnp.zeros((8, D), F32)
-    for k, part in enumerate((in_rows, out_rows, gain_rows)):
-        part = jnp.sum(part, axis=0, keepdims=True)
-        total = jnp.where(line == k, part / gain_row if k == 2 else part, total)
+        return in_rows
+
     def vector_send(stage):
         if stage == "core":
             remote(v_core.at[me.core], v_core.at[me.core], v_send.at[0], v_recv.at[0], me.partner).start()
@@ -241,12 +236,6 @@
         n = "xyz".index(stage)
         arrived(v_axes.at[n, pl.ds(0, 3)], v_recv.at[1 + n])
         return (v_axes[n, 0] + v_axes[n, 1]) + (v_axes[n, 2] + v_axes[n, 3])
-
-    if comm:
-        v_core[me.core] = total
-        vector_send("core")
-    else:
-        vectors[...] = total
 
     def matrix_send(m, stage, copies):
         for copy in copies:
@@ -334,8 +323,31 @@
     def stage_6(m):
         matrix_wait(m, 5)
 
+    zero = jnp.zeros((8, D), F32)
+    sums = (zero, zero)
+    for c in range(n_chunks):
+        sums = forward(c, sums)
+    gain_rows, out_rows = sums
     gradient(OUT, lambda at: dot(act[:, pl.ds(at, HALF)], d_mix[...], (0, 0)))
-    q[...] = dot(onehot_t[...], d_pre[...]).astype(BF16)
+    in_rows = zero
+    for c in range(n_chunks):
+        in_rows = backward(c, in_rows)
+
+    line = lax.broadcasted_iota(jnp.int32, (8, D), 0)
+    total = jnp.zeros((8, D), F32)
+    for k, part in enumerate((in_rows, out_rows, gain_rows)):
+        part = jnp.sum(part, axis=0, keepdims=True)
+        total = jnp.where(line == k, part / gain_row if k == 2 else part, total)
+    if comm:
+        v_core[me.core] = total
+        vector_send("core")
+    else:
+        vectors[...] = total
+
+    if comm:
+        stage_1(OUT)
+    final = pl.ds(EDGE - CHUNK, CHUNK)
+    q[...] = (acc_q[...] + dot(onehot_t[:, final], d_pre[final])).astype(BF16)
     gradient(SENDERS_IN, lambda at: dot(ext[:, pl.ds(at, HALF)], q[:EXT], (0, 0)))
     gradient(RECEIVERS_IN, lambda at: dot(ext[:NODE, pl.ds(at, HALF)], q[EXT:], (0, 0)))
     back_out[...] = dot(q[NODE:EXT], w_in[D : 2 * D], (1, 1)).astype(BF16)
@@ -345,12 +357,11 @@
         for k in range(4)
     ]
     if comm:
-        stage_1(OUT)
         for copy in back_copies:
             copy.start()
     else:
         back[...] = back_out[...]
-    gradient(EDGES_IN, lambda at: dot(edge[:, pl.ds(at, HALF)], d_pre[...], (0, 0)))
+    gradient(EDGES_IN, lambda at: acc_edge[pl.ds(at, HALF)] + dot(edge[final, pl.ds(at, HALF)], d_pre[final], (0, 0)))
     if comm:
         stage_1(SENDERS_IN)
         stage_1(RECEIVERS_IN)
@@ -425,6 +436,7 @@
             dma((2,)), dma((2,)),
             V((EDGE, TABLE), BF16), V((TABLE, EDGE), BF16), V((NODE, 4 * HALO), BF16), V((TABLE, D), BF16),
             V((EDGE, D), F32), V((EDGE, D), BF16), V((2, CHUNK, D), F32), V((2, CHUNK, D), F32), V((2, CHUNK, D), F32), V((2, CHUNK, D), F32),
+            V((D, D), F32), V((TABLE, D), F32),
             V((EDGE, D), BF16), V((EDGE, D), BF16),
             V((TABLE, D), BF16), V((NODE, D), F32),
             V((4, HALF, D), F32), V((4, HALF, D), BF16), V((4, HALF, D), BF16), V((4, HALF, D), BF16),
@@ -446,6 +458,9 @@
     copies = [
         pltpu.make_async_copy(edge_grad, edge_grad_hbm, sem.at[0]),
         pltpu.make_async_copy(node_grad, node_grad_hbm, sem.at[1]),
+        pltpu.make_async_copy(vectors.at[pl.ds(0, 1)], b_in_out, sem.at[6]),
+        pltpu.make_async_copy(vectors.at[pl.ds(1, 1)], b_out_out, sem.at[7]),
+        pltpu.make_async_copy(vectors.at[pl.ds(2, 1)], gain_out, sem.at[8]),
     ]
     for copy in copies:
         copy.start()
@@ -454,8 +469,6 @@
         to = w_in_hbm.at[pl.ds(m * D, D)] if m < 3 else w_out_hbm
         copies.append(pltpu.make_async_copy(wide.at[m], to, sem.at[2 + m]))
         copies[-1].start()
-    for k, out in enumerate((b_in_out, b_out_out, gain_out)):
-        out[...] = vectors[k : k + 1, :]
     for copy in copies:
         copy.wait()
 
@@ -471,8 +484,8 @@
             jax.ShapeDtypeStruct((3 * D, D), F32), vector, jax.ShapeDtypeStruct((D, D), F32), vector, vector,
         ),
         in_specs=[vmem] * 5,
-        out_specs=(hbm, hbm, hbm, vmem, hbm, vmem, vmem),
-        scratch_shapes=[pltpu.VMEM((4, D, D), F32), pltpu.SemaphoreType.DMA((6,))],
+        out_specs=(hbm,) * 7,
+        scratch_shapes=[pltpu.VMEM((4, D, D), F32), pltpu.SemaphoreType.DMA((9,))],
         compiler_params=pltpu.CompilerParams(vmem_limit_bytes=12 * 2**20),
     )(*args)
 

time: 54.1 us -> 51.8 us (0.957)
  Pallas kernels: 52.7 us -> 50.4 us
    pallas_call x1, Pallas kernels: 49.3 us -> 47.5 us  [call(): pl.pallas_call(functools.partial(kernel, comm), out_shape=(V((EDGE, D), B...]
    pallas_call x1, Pallas kernels: 3.39 us -> 2.85 us  [finish(): pl.pallas_call(finish_kernel, out_shape=(jax.ShapeDtypeStruct((EDGE, D),...]
where the time goes in v5:
time: 51.8 us; the launch traced here: 51.7 us
  Pallas kernels  50.4 us (97%)
  between operations  1.29 us (2%)
    pallas_call x1, Pallas kernels, call(): pl.pallas_call(functools.partial(kernel, comm), out_shape=(V((EDGE, D), B...  47.5 us
    pallas_call x1, Pallas kernels, finish(): pl.pallas_call(finish_kernel, out_shape=(jax.ShapeDtypeStruct((EDGE, D),...  2.85 us

profile of v5, /device:TPU:1, one launch (start us, length us, event | category | flops | bytes accessed | tf_op | source)
XLA Modules:
  0.0 51.7 jit_solution(12385948874684356237)
XLA Ops:
  1.3 47.5 %shard_map.180 = (bf16[2048,512]{1,0:T(8,128)(2,1)S(1)}, bf16[256,512]{1,0:T(8,128)(2,1)S(1)}, bf16[512,512]{1,0:T(8,128)(2,1)S(1)}, bf16[3,512,512]{2,1,0:T(8,128)(2,1)S(1)}, f32[8,512]{1,0:T(8,128)S(1)}) custom-call(bf16[256,512]{1,0:T(8,128)(2,1)} %node_hbm.1, bf16[2048,512]{1,0:T(8,128)(2,1)} %edge_hbm.1, s32[16,128]{1,0:T(8,128)} %bitcast.8, ...), custom_call_target="tpu_custom_call" | custom-call | tf_op jit(solution)/shard_map/pallas_call | solution.py:423
  48.8 2.8 %shard_map.181 = (bf16[2048,512]{1,0:T(8,128)(2,1)}, bf16[256,512]{1,0:T(8,128)(2,1)}, f32[1536,512]{1,0:T(8,128)}, f32[1,512]{1,0:T(1,128)}, f32[512,512]{1,0:T...) custom-call(bf16[2048,512]{1,0:T(8,128)(2,1)S(1)} %get-tuple-element.19.edge_grad, ...), custom_call_target="tpu_custom_call" | custom-call | tf_op jit(solution)/shard_map/pallas_call | solution.py:480

commit v6 on v5

--- a/solution.py
+++ b/solution.py
@@ -84,7 +84,7 @@
     edge_grad, node_grad, sum_out, sum_in, vectors,
     count, lists, sender, receiver, b_in, b_out, gain, ext, edge, cot, w_in, w_out, ncot, load_sem,
     rows, slots, back_out, back, halo_send, halo_recv,
-    onehot, onehot_t, list_t, proj, pre0, act, slope, half, mixed_s, at_node, acc_edge, acc_q, d_mix, d_pre, q, own_table,
+    onehot, onehot_t, list_t, proj, pre0, act, slope, half, mixed_s, at_node, acc_out, acc_q, d_mix, d_pre, q, own_table,
     grads, half_out, half_in, s1, r1, h2, s2, r2, m_send, m_recv,
     v_core, v_axes, v_send, v_recv, plane_sem,
 ):
@@ -189,6 +189,8 @@
             slope[buf, r : r + SUB] = a + (0.5 * u) * (1.0 - a)
         mixed_s[buf] = dot(act[here], w_out[...])
         at_node[buf] = dot(onehot[here, EXT:], ncot[...])
+        if c:
+            acc_out[...] = dot(act[:CHUNK], d_mix[:CHUNK], (0, 0))
         for r in range(0, CHUNK, SUB):
             there = pl.ds(start + r, SUB)
             mixed = mixed_s[buf, r : r + SUB] + b_out_row
@@ -207,12 +209,6 @@
         start, buf = c * CHUNK, c
         here = pl.ds(start, CHUNK)
         half[buf] = dot(d_mix[here], w_out[...], (1, 1))
-        if c:
-            before = pl.ds(start - CHUNK, CHUNK)
-            new_edge = dot(edge[before], d_pre[before], (0, 0))
-            new_q = dot(onehot_t[:, before], d_pre[before])
-            acc_edge[...] = new_edge if c == 1 else acc_edge[...] + new_edge
-            acc_q[...] = new_q if c == 1 else acc_q[...] + new_q
         for r in range(0, CHUNK, SUB):
             there = pl.ds(start + r, SUB)
             d_p = half[buf, r : r + SUB] * slope[buf, r : r + SUB]
@@ -253,14 +249,17 @@
     mine = me.core * HALF
     theirs = HALF - mine
 
-    def gradient(m, compute):
-        first = compute(pl.multiple_of(theirs, HALF))
+    def gradient_theirs(m, compute):
+        part = compute(pl.multiple_of(theirs, HALF)).astype(BF16)
         if comm:
-            half_out[m] = first.astype(BF16)
+            half_out[m] = part
             matrix_send(m, 0, [remote(half_out.at[m], half_in.at[m], *sems(m, 0), me.partner)])
+        else:
+            sum_out[:HALF] = part
+
+    def gradient_mine(m, compute):
         grads[m] = compute(pl.multiple_of(mine, HALF))
         if not comm:
-            sum_out[:HALF] = first.astype(BF16)
             sum_out[HALF:] = grads[m].astype(BF16)
             sum_in[0] = sum_out[...]
 
@@ -328,9 +327,13 @@
     for c in range(n_chunks):
         sums = forward(c, sums)
     gain_rows, out_rows = sums
-    gradient(OUT, lambda at: dot(act[:, pl.ds(at, HALF)], d_mix[...], (0, 0)))
+    out_part = lambda at: acc_out[pl.ds(at, HALF)] + dot(act[CHUNK:, pl.ds(at, HALF)], d_mix[CHUNK:], (0, 0))
+    gradient_theirs(OUT, out_part)
+    gradient_mine(OUT, out_part)
     in_rows = zero
     for c in range(n_chunks):
+        if comm and c == 1:
+            stage_1(OUT)
         in_rows = backward(c, in_rows)
 
     line = lax.broadcasted_iota(jnp.int32, (8, D), 0)
@@ -344,12 +347,17 @@
     else:
         vectors[...] = total
 
-    if comm:
-        stage_1(OUT)
     final = pl.ds(EDGE - CHUNK, CHUNK)
-    q[...] = (acc_q[...] + dot(onehot_t[:, final], d_pre[final])).astype(BF16)
-    gradient(SENDERS_IN, lambda at: dot(ext[:, pl.ds(at, HALF)], q[:EXT], (0, 0)))
-    gradient(RECEIVERS_IN, lambda at: dot(ext[:NODE, pl.ds(at, HALF)], q[EXT:], (0, 0)))
+    q[...] = dot(onehot_t[...], d_pre[...]).astype(BF16)
+    parts = {
+        SENDERS_IN: lambda at: dot(ext[:, pl.ds(at, HALF)], q[:EXT], (0, 0)),
+        RECEIVERS_IN: lambda at: dot(ext[:NODE, pl.ds(at, HALF)], q[EXT:], (0, 0)),
+        EDGES_IN: lambda at: dot(edge[:, pl.ds(at, HALF)], d_pre[...], (0, 0)),
+    }
+    for m in (SENDERS_IN, RECEIVERS_IN):
+        gradient_theirs(m, parts[m])
+    for m in (SENDERS_IN, RECEIVERS_IN):
+        gradient_mine(m, parts[m])
     back_out[...] = dot(q[NODE:EXT], w_in[D : 2 * D], (1, 1)).astype(BF16)
     back_to = (me.west, me.east, me.south, me.north)
     back_copies = [
@@ -361,15 +369,16 @@
             copy.start()
     else:
         back[...] = back_out[...]
-    gradient(EDGES_IN, lambda at: acc_edge[pl.ds(at, HALF)] + dot(edge[final, pl.ds(at, HALF)], d_pre[final], (0, 0)))
+    gradient_theirs(EDGES_IN, parts[EDGES_IN])
     if comm:
         stage_1(SENDERS_IN)
         stage_1(RECEIVERS_IN)
+    gradient_mine(EDGES_IN, parts[EDGES_IN])
+    if comm:
+        stage_1(EDGES_IN)
         v_axes[0, me.lat] = vector_sum("core")
         vector_send("x")
     own_table[...] = dot(q[:NODE], w_in[D : 2 * D], (1, 1)) + dot(q[EXT:], w_in[2 * D :], (1, 1))
-    if comm:
-        stage_1(EDGES_IN)
 
     def last(c, _):
         here = rows_at(c * CHUNK, CHUNK, CHUNK)

time: 51.8 us -> 51.1 us (0.986)
  Pallas kernels: 50.4 us -> 49.6 us
    pallas_call x1, Pallas kernels: 47.5 us -> 46.8 us  [call(): pl.pallas_call(functools.partial(kernel, comm), out_shape=(V((EDGE, D), B...]
where the time goes in v6:
time: 51.1 us; the launch traced here: 50.9 us
  Pallas kernels  49.6 us (97%)
  between operations  1.29 us (3%)
    pallas_call x1, Pallas kernels, call(): pl.pallas_call(functools.partial(kernel, comm), out_shape=(V((EDGE, D), B...  46.8 us
    pallas_call x1, Pallas kernels, finish(): pl.pallas_call(finish_kernel, out_shape=(jax.ShapeDtypeStruct((EDGE, D),...  2.85 us

profile of v6, /device:TPU:1, one launch (start us, length us, event | category | flops | bytes accessed | tf_op | source)
XLA Modules:
  0.0 50.9 jit_solution(2050030178902177848)
XLA Ops:
  1.3 46.8 %shard_map.180 = (bf16[2048,512]{1,0:T(8,128)(2,1)S(1)}, bf16[256,512]{1,0:T(8,128)(2,1)S(1)}, bf16[512,512]{1,0:T(8,128)(2,1)S(1)}, bf16[3,512,512]{2,1,0:T(8,128)(2,1)S(1)}, f32[8,512]{1,0:T(8,128)S(1)}) custom-call(bf16[256,512]{1,0:T(8,128)(2,1)} %node_hbm.1, bf16[2048,512]{1,0:T(8,128)(2,1)} %edge_hbm.1, s32[16,128]{1,0:T(8,128)} %bitcast.8, ...), custom_call_target="tpu_custom_call" | custom-call | tf_op jit(solution)/shard_map/pallas_call | solution.py:432
  48.1 2.8 %shard_map.181 = (bf16[2048,512]{1,0:T(8,128)(2,1)}, bf16[256,512]{1,0:T(8,128)(2,1)}, f32[1536,512]{1,0:T(8,128)}, f32[1,512]{1,0:T(1,128)}, f32[512,512]{1,0:T...) custom-call(bf16[2048,512]{1,0:T(8,128)(2,1)S(1)} %get-tuple-element.19.edge_grad, ...), custom_call_target="tpu_custom_call" | custom-call | tf_op jit(solution)/shard_map/pallas_call | solution.py:489
